TPU v7x, 256 devices: a whole 4x4x8 slice. The times are simulated.
256 devices in a mesh: ctx: 64 (over y, x_hi, z), head: 4 (over x_lo, core).
Axes of the slice: x: 4 (x_hi: 2, x_lo: 2; x = x_hi * 2 + x_lo), y: 4, z: 8, core: 2. Of those that a mesh axis runs over, the one named last changes fastest.
Arguments:
- query_input: bfloat16 [16384, 4096], P('ctx', 'head'), may hold values from -6 to 6
- key_entries_raw: bfloat16 [16384, 1024], P('ctx', 'head'), may hold values from -6 to 6
- value_entries_raw: bfloat16 [16384, 1024], P('ctx', 'head'), may hold values from -6 to 6
- out_grad: bfloat16 [16384, 4096], P('ctx', 'head'), may hold values from -6 to 6
- attn_out: bfloat16 [16384, 4096], P('ctx', 'head'), may hold values from -3 to 3
- log_sum_exp: float32 [32, 16384], P('head', 'ctx'), may hold values from 4 to 6
- positions: int32 [3, 16384], P(None, ('ctx', 'head')), may hold values from 0 to 4095
- span_map: int32 [64], replicated, may hold values from 0 to 63, each once
Outputs:
- query_grad: bfloat16 [16384, 4096], P('ctx', 'head')
- key_gradient_raw: bfloat16 [16384, 1024], P('ctx', 'head')
- value_gradient_rows: bfloat16 [16384, 1024], P('ctx', 'head')
Inputs may be any that keep to these rules, and one draw needn't show every extreme that they name: Block b of 256 rows holds span span_map[b] of the sequence in its first 128 rows and span 2 * 64 - 1 - span_map[b] in its last 128 rows; each number appears once.
All inputs are finite; a program needn't handle non-finite values.
Results may differ from a plain program's by a relative error of at most 0.019.
The roundings to bfloat16 on the way count: a program that leaves them out, or rounds other values in their place, can miss the bound.
Values may be sent and summed in bfloat16 or wider, within the bound.
A program may use at most 64 MiB of HBM per device.

v0:
```python
import math

import jax
import jax.numpy as jnp
from jax import lax
from jax.sharding import PartitionSpec as P

HEAD_ENTRIES = 128
WIN = 4


ROPE_BASE = 1000000.0
YARN_FACTOR = 4.0
YARN_INITIAL = 32768.0
BETA_FAST = 32.0
BETA_SLOW = 1.0
YARN_MSCALE = 1.0 + 0.1 * math.log(4.0)


def shifted(value, axis, steps):
    count = lax.axis_size(axis)
    pairs = [(source, (source + steps) % count) for source in range(count)]
    return lax.ppermute(value, axis, pairs)


def rope_tables(positions, head_width):
    half_width = head_width // 2
    pair_index = jnp.arange(half_width, dtype=jnp.float32)
    inverse = jnp.exp(-2.0 * pair_index / head_width * math.log(ROPE_BASE))
    ratio_value = YARN_INITIAL * inverse / (2.0 * math.pi)
    ramp_value = jnp.clip((ratio_value - BETA_SLOW) / (BETA_FAST - BETA_SLOW), 0.0, 1.0)
    frequency = inverse * ((1.0 - ramp_value) / YARN_FACTOR + ramp_value)
    first_cut = head_width // 8
    second_cut = first_cut + 3 * head_width // 16
    spot_values = positions.astype(jnp.float32)
    chosen = jnp.where(
        pair_index < first_cut,
        spot_values[0][:, None],
        jnp.where(pair_index < second_cut, spot_values[1][:, None], spot_values[2][:, None]),
    )
    angles = chosen * frequency
    return (jnp.cos(angles) * YARN_MSCALE, jnp.sin(angles) * YARN_MSCALE)


def apply_rotary(block_rows, cosine_lookup, sine_lookup):
    half_width = block_rows.shape[-1] // 2
    widened = block_rows.astype(jnp.float32)
    first_half = widened[..., :half_width]
    second_half = widened[..., half_width:]
    cosine_rows = cosine_lookup[:, None, :]
    sine_rows = sine_lookup[:, None, :]
    return jnp.concatenate(
        [
            first_half * cosine_rows - second_half * sine_rows,
            second_half * cosine_rows + first_half * sine_rows,
        ],
        axis=-1,
    )


def reverse_rotary(gradient, cosine_lookup, sine_lookup):
    half_width = gradient.shape[-1] // 2
    first_half = gradient[..., :half_width]
    second_half = gradient[..., half_width:]
    cosine_rows = cosine_lookup[:, None, :]
    sine_rows = sine_lookup[:, None, :]
    return jnp.concatenate(
        [
            first_half * cosine_rows + second_half * sine_rows,
            second_half * cosine_rows - first_half * sine_rows,
        ],
        axis=-1,
    )


def slot_order(span_map, slot_index, span_len, cycle_size):
    early_span = span_map[slot_index]
    late_span = 2 * cycle_size - 1 - early_span
    offsets = jnp.arange(span_len, dtype=jnp.int32)
    return jnp.concatenate([early_span * span_len + offsets, late_span * span_len + offsets])


def block_grads(query_side, key_side, query_order, key_order):
    query_rotated, grad_heads, norm_rows, delta_rows = query_side
    key_turned, value_head_split = key_side
    row_count = query_rotated.shape[0]
    key_heads = key_turned.shape[1]
    head_width = key_turned.shape[2]
    group_size = query_rotated.shape[1] // key_heads
    root_scale = 1.0 / math.sqrt(head_width)
    query_groups = query_rotated.reshape(row_count, key_heads, group_size, head_width)
    grad_groups = grad_heads.reshape(row_count, key_heads, group_size, head_width)
    scores = (
        jnp.einsum("qgjd,kgd->gjqk", query_groups, key_turned, preferred_element_type=jnp.float32)
        * root_scale
    )
    visible = key_order[None, :] <= query_order[:, None]
    norm_table = norm_rows.reshape(key_heads, group_size, row_count)[..., None]
    weights = jnp.where(visible, jnp.exp(scores - norm_table), 0.0)
    rounded_weights = weights.astype(jnp.bfloat16)
    value_part = jnp.einsum(
        "gjqk,qgjd->kgd", rounded_weights, grad_groups, preferred_element_type=jnp.float32
    )
    weight_grad = jnp.einsum(
        "qgjd,kgd->gjqk", grad_groups, value_head_split, preferred_element_type=jnp.float32
    )
    score_grad = weights * (
        weight_grad - delta_rows.reshape(key_heads, group_size, row_count)[..., None]
    )
    rounded_grad = score_grad.astype(jnp.bfloat16)
    key_part = (
        jnp.einsum("gjqk,qgjd->kgd", rounded_grad, query_groups, preferred_element_type=jnp.float32)
        * root_scale
    )
    query_part = jnp.einsum(
        "gjqk,kgd->qgjd", rounded_grad, key_turned, preferred_element_type=jnp.float32
    )
    query_part = query_part.reshape(row_count, key_heads * group_size, head_width) * root_scale
    return (query_part, key_part, value_part)


def pair_grads(query_side, key_side, query_order, key_order):
    pieces = block_grads(query_side, key_side, query_order, key_order)
    return pieces


def shards(
    query_input,
    key_entries_raw,
    value_entries_raw,
    out_grad,
    attn_out,
    log_sum_exp,
    positions,
    span_map,
):
    row_count = query_input.shape[0]
    span_len = row_count // 2
    query_heads = query_input.shape[1] // HEAD_ENTRIES
    key_heads = key_entries_raw.shape[1] // HEAD_ENTRIES
    cycle_size = lax.axis_size("ctx")
    self_slot = lax.axis_index("ctx")
    placed = lax.all_gather(positions, "head", axis=1, tiled=True)
    cosine_lookup, sine_lookup = rope_tables(placed, HEAD_ENTRIES)
    query_rotated = apply_rotary(
        query_input.reshape(row_count, query_heads, HEAD_ENTRIES), cosine_lookup, sine_lookup
    ).astype(jnp.bfloat16)
    key_turned = apply_rotary(
        key_entries_raw.reshape(row_count, key_heads, HEAD_ENTRIES), cosine_lookup, sine_lookup
    ).astype(jnp.bfloat16)
    value_head_split = value_entries_raw.reshape(row_count, key_heads, HEAD_ENTRIES)
    grad_heads = out_grad.reshape(row_count, query_heads, HEAD_ENTRIES)
    delta_rows = jnp.sum(
        grad_heads.astype(jnp.float32)
        * attn_out.reshape(row_count, query_heads, HEAD_ENTRIES).astype(jnp.float32),
        axis=2,
    ).T
    self_order = slot_order(span_map, self_slot, span_len, cycle_size)
    moving_query = query_rotated
    moving_grad = grad_heads
    moving_norm = log_sum_exp
    moving_delta = delta_rows
    carried = jnp.zeros((row_count, query_heads, HEAD_ENTRIES), jnp.float32)
    key_overall = jnp.zeros((row_count, key_heads, HEAD_ENTRIES), jnp.float32)
    value_overall = jnp.zeros((row_count, key_heads, HEAD_ENTRIES), jnp.float32)
    for hop_index in range(WIN):
        if hop_index > 0:
            moving_query, moving_grad = shifted((moving_query, moving_grad), "ctx", 1)
            carried, moving_norm, moving_delta = shifted(
                (carried, moving_norm, moving_delta), "ctx", 1
            )
        source = (self_slot - hop_index) % cycle_size
        source_order = slot_order(span_map, source, span_len, cycle_size)
        pieces = pair_grads(
            (moving_query, moving_grad, moving_norm, moving_delta),
            (key_turned, value_head_split),
            source_order,
            self_order,
        )
        carried = carried + pieces[0]
        key_overall = key_overall + pieces[1]
        value_overall = value_overall + pieces[2]
    query_total = shifted(carried, "ctx", 1 - WIN)
    query_grad = (
        reverse_rotary(query_total, cosine_lookup, sine_lookup)
        .reshape(row_count, query_heads * HEAD_ENTRIES)
        .astype(jnp.bfloat16)
    )
    key_gradient_raw = (
        reverse_rotary(key_overall, cosine_lookup, sine_lookup)
        .reshape(row_count, key_heads * HEAD_ENTRIES)
        .astype(jnp.bfloat16)
    )
    value_gradient_rows = value_overall.reshape(row_count, key_heads * HEAD_ENTRIES).astype(
        jnp.bfloat16
    )
    return (query_grad, key_gradient_raw, value_gradient_rows)


def solution(mesh):
    placed = (
        P("ctx", "head"),
        P("ctx", "head"),
        P("ctx", "head"),
        P("ctx", "head"),
        P("ctx", "head"),
        P("head", "ctx"),
        P(None, ("ctx", "head")),
        P(),
    )
    return jax.shard_map(
        shards,
        mesh=mesh,
        in_specs=placed,
        out_specs=(P("ctx", "head"), P("ctx", "head"), P("ctx", "head")),
        check_vma=False,
    )
```

profile of v0, /device:TPU:2, one launch (start us, length us, event | category | flops | bytes accessed | tf_op | source)
XLA Modules:
  0.0 254.9 jit_solution(6538723871126055212)
XLA Ops:
  0.6 2.0 collective-permute-start.2
  2.6 1.9 copy.332
  4.6 1.9 collective-permute-start.3
  7.9 2.1 multiply_reduce_fusion
  11.9 5.4 %all-gather = s32[4,64,3]{1,2,0:T(4,128)S(1)} all-gather(s32[1,64,3]{1,2,0:T(4,128)S(1)} %bitcast.243), channel_id=1, replica_groups=mesh['ctx'=64,'head'=4] {'head'}, dimensions={0}, use_global_device_ids=true | all-gather | bytes 3840 | tf_op jit(solution)/shard_map/all_gather | solution.py:143
  20.2 2.9 %collective-permute-start.1 = (bf16[256,8,128]{2,0,1:T(8,128)(2,1)}, bf16[256,8,128]{2,0,1:T(8,128)(2,1)}, u32[]{:S(2)}, u32[]{:S(2)}) collective-permute-start(bf16[256,8,128]{2,0,1:T(8,128)(2,1)} %pad_maximum_fusion.1), channel_id=1, source_target_pairs={{0,4},{4,8},{8,12},{12,16},{16,20},{20,24},{24,28},{28,32},{32,36}... | collective-permute-start | bytes 1572872 | tf_op jit(solution)/shard_map/ppermute | solution.py:23
  37.7 2.5 copy.220
  43.3 2.3 convolution_bitcast_fusion.7
  45.6 26.8 %collective-permute-done.7 = f32[8,256]{1,0:T(8,128)S(1)} collective-permute-done((f32[8,256]{1,0:T(8,128)}, f32[8,256]{1,0:T(8,128)S(1)}, u32[]{:S(2)}, u32[]{:S(2)}) %collective-permute-start.7) | collective-permute-done | bytes 8224 | tf_op jit(solution)/shard_map/ppermute | solution.py:23
  72.4 2.0 collective-permute-done.9
  79.5 5.7 %collective-permute-done.14 = f32[8,256]{0,1:T(8,128)S(1)} collective-permute-done((f32[8,256]{0,1:T(8,128)}, f32[8,256]{0,1:T(8,128)S(1)}, u32[]{:S(2)}, u32[]{:S(2)}) %collective-permute-start.14) | collective-permute-done | bytes 8224 | tf_op jit(solution)/shard_map/ppermute | solution.py:23
  90.1 3.2 %fusion.19 = f32[2,256,128]{1,2,0:T(8,128)} fusion(f32[2,256,128]{1,2,0:T(8,128)} %convolution_bitcast_fusion.7, bf16[256,2,4,128]{3,0,2,1:T(8,128)(2,1)} %bitcast.232, f32[2,256,256,4]{2,1,3,0:T(8,128)} %copy-done.7, f32[2,4,256]{2,1,0:T(4,128)} %copy-done.36, pred[256,256]{0,1:T(8,128)(4,1)} %get-tuple-element.36), kind=kOutput, calls=%fused_computation.39 | convolution fusion | flops 136380416 | bytes 3219456 | tf_op jit(solution)/shard_map/gjqk,qgjd->kgd/dot_general | solution.py:101
  93.2 2.4 add.170
  95.6 2.2 fusion.22
  97.8 13.1 %collective-permute-done.8 = bf16[256,8,128]{2,1,0:T(8,128)(2,1)} collective-permute-done((bf16[256,8,128]{2,1,0:T(8,128)(2,1)}, bf16[256,8,128]{2,1,0:T(8,128)(2,1)}, u32[]{:S(2)}, u32[]{:S(2)}) %collective-permute-start.8) | collective-permute-done | bytes 524320 | tf_op jit(solution)/shard_map/ppermute | solution.py:23
  112.1 10.0 %collective-permute-done.6 = bf16[256,8,128]{2,0,1:T(8,128)(2,1)} collective-permute-done((bf16[256,8,128]{2,0,1:T(8,128)(2,1)}, bf16[256,8,128]{2,0,1:T(8,128)(2,1)}, u32[]{:S(2)}, u32[]{:S(2)}) %collective-permute-start.6) | collective-permute-done | bytes 524320 | tf_op jit(solution)/shard_map/ppermute | solution.py:23
  125.7 18.9 %collective-permute-done.5 = f32[256,8,128]{2,0,1:T(8,128)} collective-permute-done((f32[256,8,128]{2,0,1:T(8,128)}, f32[256,8,128]{2,0,1:T(8,128)}, u32[]{:S(2)}, u32[]{:S(2)}) %collective-permute-start.5) | collective-permute-done | bytes 1048608 | tf_op jit(solution)/shard_map/ppermute | solution.py:23
  144.6 2.3 add.177
  148.3 7.5 %collective-permute-done.13 = bf16[256,8,128]{2,1,0:T(8,128)(2,1)} collective-permute-done((bf16[256,8,128]{2,1,0:T(8,128)(2,1)}, bf16[256,8,128]{2,1,0:T(8,128)(2,1)}, u32[]{:S(2)}, u32[]{:S(2)}) %collective-permute-start.13) | collective-permute-done | bytes 524320 | tf_op jit(solution)/shard_map/ppermute | solution.py:23
  156.9 10.1 %collective-permute-done.11 = bf16[256,8,128]{2,0,1:T(8,128)(2,1)} collective-permute-done((bf16[256,8,128]{2,0,1:T(8,128)(2,1)}, bf16[256,8,128]{2,0,1:T(8,128)(2,1)}, u32[]{:S(2)}, u32[]{:S(2)}) %collective-permute-start.11) | collective-permute-done | bytes 524320 | tf_op jit(solution)/shard_map/ppermute | solution.py:23
  172.8 13.7 %collective-permute-done.10 = f32[256,8,128]{2,0,1:T(8,128)} collective-permute-done((f32[256,8,128]{2,0,1:T(8,128)}, f32[256,8,128]{2,0,1:T(8,128)}, u32[]{:S(2)}, u32[]{:S(2)}) %collective-permute-start.10) | collective-permute-done | bytes 1048608 | tf_op jit(solution)/shard_map/ppermute | solution.py:23
  186.5 2.3 add.184
  188.8 2.2 fusion.23
  195.0 58.3 %collective-permute-done.15 = f32[256,8,128]{2,0,1:T(8,128)S(1)} collective-permute-done((f32[256,8,128]{2,0,1:T(8,128)}, f32[256,8,128]{2,0,1:T(8,128)S(1)}, u32[]{:S(2)}, u32[]{:S(2)}) %collective-permute-start.15) | collective-permute-done | bytes 1048608 | tf_op jit(solution)/shard_map/ppermute | solution.py:23
  (173 shorter events, 45.5 us)
Async XLA Ops:
  0.6 40.6 %collective-permute-start.2 = (f32[8,256]{1,0:T(8,128)}, f32[8,256]{1,0:T(8,128)}, u32[]{:S(2)}, u32[]{:S(2)}) collective-permute-start(f32[8,256]{1,0:T(8,128)} %param.13), channel_id=1, source_target_pairs={{0,4},{4,8},{8,12},{12,16},{16,20},{20,24},{24,28},{28,32},{32,36}... | collective-permute-start | bytes 24584 | tf_op jit(solution)/shard_map/ppermute | solution.py:23
  4.6 82.3 %collective-permute-start.3 = (bf16[256,8,128]{2,1,0:T(8,128)(2,1)}, bf16[256,8,128]{2,1,0:T(8,128)(2,1)}, u32[]{:S(2)}, u32[]{:S(2)}) collective-permute-start(bf16[256,8,128]{2,1,0:T(8,128)(2,1)} %bitcast.91), channel_id=1, source_target_pairs={{0,4},{4,8},{8,12},{12,16},{16,20},{20,24},{24,28},{28,32},{32,36}... | collective-permute-start | bytes 1572872 | tf_op jit(solution)/shard_map/ppermute | solution.py:23
  9.9 32.4 %collective-permute-start.4 = (f32[8,256]{0,1:T(8,128)}, f32[8,256]{0,1:T(8,128)}, u32[]{:S(2)}, u32[]{:S(2)}) collective-permute-start(f32[8,256]{0,1:T(8,128)} %bitcast.20), channel_id=1, source_target_pairs={{0,4},{4,8},{8,12},{12,16},{16,20},{20,24},{24,28},{28,32},{32,36}... | collective-permute-start | bytes 24584 | tf_op jit(solution)/shard_map/ppermute | solution.py:23
  20.2 65.1 %collective-permute-start.1 = (bf16[256,8,128]{2,0,1:T(8,128)(2,1)}, bf16[256,8,128]{2,0,1:T(8,128)(2,1)}, u32[]{:S(2)}, u32[]{:S(2)}) collective-permute-start(bf16[256,8,128]{2,0,1:T(8,128)(2,1)} %pad_maximum_fusion.1), channel_id=1, source_target_pairs={{0,4},{4,8},{8,12},{12,16},{16,20},{20,24},{24,28},{28,32},{32,36}... | collective-permute-start | bytes 1572872 | tf_op jit(solution)/shard_map/ppermute | solution.py:23
  40.2 34.1 %copy-start.1 = (bf16[256,8,64]{2,0,1:T(8,128)(2,1)S(1)}, bf16[256,8,64]{2,0,1:T(8,128)(2,1)}, u32[]{:S(2)}) copy-start(bf16[256,8,64]{2,0,1:T(8,128)(2,1)} %copy-done) | copy-start | bytes 786436
  40.2 34.1 %copy-start.3 = (bf16[256,8,64]{2,0,1:T(8,128)(2,1)S(1)}, bf16[256,8,64]{2,0,1:T(8,128)(2,1)}, u32[]{:S(2)}) copy-start(bf16[256,8,64]{2,0,1:T(8,128)(2,1)} %copy-done.2) | copy-start | bytes 786436
  40.2 53.0 %collective-permute-start = (f32[256,8,128]{2,0,1:T(8,128)}, f32[256,8,128]{2,0,1:T(8,128)}, u32[]{:S(2)}, u32[]{:S(2)}) collective-permute-start(f32[256,8,128]{2,0,1:T(8,128)} %copy.220), channel_id=1, source_target_pairs={{0,4},{4,8},{8,12},{12,16},{16,20},{20,24},{24,28},{28,32},{32,36}... | collective-permute-start | bytes 3145736 | tf_op jit(solution)/shard_map/ppermute | solution.py:23
  41.3 31.1 %collective-permute-start.7 = (f32[8,256]{1,0:T(8,128)}, f32[8,256]{1,0:T(8,128)S(1)}, u32[]{:S(2)}, u32[]{:S(2)}) collective-permute-start(f32[8,256]{1,0:T(8,128)} %collective-permute-done.2), channel_id=1, source_target_pairs={{0,4},{4,8},{8,12},{12,16},{16,20},{20,24},{24,28},{28,32},{32,36}... | collective-permute-start | bytes 24584 | tf_op jit(solution)/shard_map/ppermute | solution.py:23
  42.3 32.1 %collective-permute-start.9 = (f32[8,256]{0,1:T(8,128)}, f32[8,256]{0,1:T(8,128)}, u32[]{:S(2)}, u32[]{:S(2)}) collective-permute-start(f32[8,256]{0,1:T(8,128)} %collective-permute-done.4), channel_id=1, source_target_pairs={{0,4},{4,8},{8,12},{12,16},{16,20},{20,24},{24,28},{28,32},{32,36}... | collective-permute-start | bytes 24584 | tf_op jit(solution)/shard_map/ppermute | solution.py:23
  72.4 13.0 %collective-permute-start.12 = (f32[8,256]{1,0:T(8,128)S(1)}, f32[8,256]{1,0:T(8,128)S(1)}, u32[]{:S(2)}, u32[]{:S(2)}) collective-permute-start(f32[8,256]{1,0:T(8,128)S(1)} %collective-permute-done.7), channel_id=1, source_target_pairs={{0,4},{4,8},{8,12},{12,16},{16,20},{20,24},{24,28},{28,32},{32,36}... | collective-permute-start | bytes 24584 | tf_op jit(solution)/shard_map/ppermute | solution.py:23
  74.4 10.9 %collective-permute-start.14 = (f32[8,256]{0,1:T(8,128)}, f32[8,256]{0,1:T(8,128)S(1)}, u32[]{:S(2)}, u32[]{:S(2)}) collective-permute-start(f32[8,256]{0,1:T(8,128)} %collective-permute-done.9), channel_id=1, source_target_pairs={{0,4},{4,8},{8,12},{12,16},{16,20},{20,24},{24,28},{28,32},{32,36}... | collective-permute-start | bytes 24584 | tf_op jit(solution)/shard_map/ppermute | solution.py:23
  89.9 21.0 %collective-permute-start.8 = (bf16[256,8,128]{2,1,0:T(8,128)(2,1)}, bf16[256,8,128]{2,1,0:T(8,128)(2,1)}, u32[]{:S(2)}, u32[]{:S(2)}) collective-permute-start(bf16[256,8,128]{2,1,0:T(8,128)(2,1)} %collective-permute-done.3), channel_id=1, source_target_pairs={{0,4},{4,8},{8,12},{12,16},{16,20},{20,24},{24,28},{28,32},{32,36}... | collective-permute-start | bytes 1572872 | tf_op jit(solution)/shard_map/ppermute | solution.py:23
  90.0 32.1 %collective-permute-start.6 = (bf16[256,8,128]{2,0,1:T(8,128)(2,1)}, bf16[256,8,128]{2,0,1:T(8,128)(2,1)}, u32[]{:S(2)}, u32[]{:S(2)}) collective-permute-start(bf16[256,8,128]{2,0,1:T(8,128)(2,1)} %collective-permute-done.1), channel_id=1, source_target_pairs={{0,4},{4,8},{8,12},{12,16},{16,20},{20,24},{24,28},{28,32},{32,36}... | collective-permute-start | bytes 1572872 | tf_op jit(solution)/shard_map/ppermute | solution.py:23
  95.6 49.0 %collective-permute-start.5 = (f32[256,8,128]{2,0,1:T(8,128)}, f32[256,8,128]{2,0,1:T(8,128)}, u32[]{:S(2)}, u32[]{:S(2)}) collective-permute-start(f32[256,8,128]{2,0,1:T(8,128)} %add.170), channel_id=1, source_target_pairs={{0,4},{4,8},{8,12},{12,16},{16,20},{20,24},{24,28},{28,32},{32,36}... | collective-permute-start | bytes 3145736 | tf_op jit(solution)/shard_map/ppermute | solution.py:23
  97.8 25.9 %copy-start.22 = (bf16[256,2,128]{2,1,0:T(2,128)(2,1)S(1)}, bf16[256,2,128]{2,1,0:T(2,128)(2,1)}, u32[]{:S(2)}) copy-start(bf16[256,2,128]{2,1,0:T(2,128)(2,1)} %reshape.264) | copy-start | bytes 393220
  97.8 25.9 %copy-start.27 = (pred[256,256]{0,1:T(8,128)(4,1)S(1)}, pred[256,256]{0,1:T(8,128)(4,1)}, u32[]{:S(2)}) copy-start(pred[256,256]{0,1:T(8,128)(4,1)} %get-tuple-element.37) | copy-start | bytes 196612
  97.8 25.9 %copy-start.32 = (f32[2,4,256]{2,1,0:T(4,128)S(1)}, f32[2,4,256]{2,1,0:T(4,128)}, u32[]{:S(2)}) copy-start(f32[2,4,256]{2,1,0:T(4,128)} %sub.153) | copy-start | bytes 24580
  97.8 25.9 %copy-start.35 = (f32[2,4,256]{2,1,0:T(4,128)S(1)}, f32[2,4,256]{2,1,0:T(4,128)}, u32[]{:S(2)}) copy-start(f32[2,4,256]{2,1,0:T(4,128)} %sub.156) | copy-start | bytes 24580
  112.0 43.8 %collective-permute-start.13 = (bf16[256,8,128]{2,1,0:T(8,128)(2,1)}, bf16[256,8,128]{2,1,0:T(8,128)(2,1)}, u32[]{:S(2)}, u32[]{:S(2)}) collective-permute-start(bf16[256,8,128]{2,1,0:T(8,128)(2,1)} %collective-permute-done.8), channel_id=1, source_target_pairs={{0,4},{4,8},{8,12},{12,16},{16,20},{20,24},{24,28},{28,32},{32,36}... | collective-permute-start | bytes 1572872 | tf_op jit(solution)/shard_map/ppermute | solution.py:23
  122.1 44.9 %collective-permute-start.11 = (bf16[256,8,128]{2,0,1:T(8,128)(2,1)}, bf16[256,8,128]{2,0,1:T(8,128)(2,1)}, u32[]{:S(2)}, u32[]{:S(2)}) collective-permute-start(bf16[256,8,128]{2,0,1:T(8,128)(2,1)} %collective-permute-done.6), channel_id=1, source_target_pairs={{0,4},{4,8},{8,12},{12,16},{16,20},{20,24},{24,28},{28,32},{32,36}... | collective-permute-start | bytes 1572872 | tf_op jit(solution)/shard_map/ppermute | solution.py:23
  125.6 21.2 %copy-start.9 = (f32[2,256,256,4]{2,1,3,0:T(8,128)S(1)}, f32[2,256,256,4]{2,1,3,0:T(8,128)}, u32[]{:S(2)}) copy-start(f32[2,256,256,4]{2,1,3,0:T(8,128)} %copy-done.8) | copy-start | bytes 6291460
  125.7 21.2 %copy-start.16 = (bf16[256,8,128]{2,0,1:T(8,128)(2,1)S(1)}, bf16[256,8,128]{2,0,1:T(8,128)(2,1)}, u32[]{:S(2)}) copy-start(bf16[256,8,128]{2,0,1:T(8,128)(2,1)} %copy-done.15) | copy-start | bytes 1572868
  146.9 39.6 %collective-permute-start.10 = (f32[256,8,128]{2,0,1:T(8,128)}, f32[256,8,128]{2,0,1:T(8,128)}, u32[]{:S(2)}, u32[]{:S(2)}) collective-permute-start(f32[256,8,128]{2,0,1:T(8,128)} %add.177), channel_id=1, source_target_pairs={{0,4},{4,8},{8,12},{12,16},{16,20},{20,24},{24,28},{28,32},{32,36}... | collective-permute-start | bytes 3145736 | tf_op jit(solution)/shard_map/ppermute | solution.py:23
  188.8 64.5 %collective-permute-start.15 = (f32[256,8,128]{2,0,1:T(8,128)}, f32[256,8,128]{2,0,1:T(8,128)S(1)}, u32[]{:S(2)}, u32[]{:S(2)}) collective-permute-start(f32[256,8,128]{2,0,1:T(8,128)} %add.184), channel_id=1, source_target_pairs={{0,244},{4,248},{8,252},{12,0},{16,4},{20,8},{24,12},{28,16},{32,2... | collective-permute-start | bytes 3145736 | tf_op jit(solution)/shard_map/ppermute | solution.py:23
  (32 other events, 353.5 us)
where the time goes:
time: 256 us; the launch traced here: 255 us
  waiting for transfers between devices  166 us (65%)
  matrix products  25.7 us (10%)
  local copies, waits for them, and re-layouts  22.5 us (9%)
  other arithmetic  15.4 us (6%)
  starting transfers between devices  12.1 us (5%)
  between operations  7.73 us (3%)
  blocking collectives  5.35 us (2%)
    ppermute x16, waiting for transfers between devices, shifted(): return lax.ppermute(value, axis, pairs)  166 us
    ppermute x16, starting transfers between devices, shifted(): return lax.ppermute(value, axis, pairs)  12.1 us
    dot_general x4, matrix products, block_grads(): jnp.einsum('gjqk,qgjd->kgd', rounded_weights, grad_groups, preferred_elem...  7.42 us
    dot_general x4, matrix products, block_grads(): jnp.einsum('gjqk,qgjd->kgd', rounded_grad, query_groups, preferred_elemen...  7.03 us
    add x3, other arithmetic, shards(): carried = carried + pieces[0]  6.97 us
    ppermute x6, local copies, waits for them, and re-layouts, shifted(): return lax.ppermute(value, axis, pairs)  5.72 us
    unnamed x88, local copies, waits for them, and re-layouts  5.56 us
    all_gather x1, blocking collectives, shards(): placed = lax.all_gather(positions, 'head', axis=1, tiled=True)  5.35 us
  transfers between devices with their start and end apart: 16, of which 10 were waited for; matrix products, arithmetic and copies ran while one was open for 23% of the time, Pallas kernels for 0%

commit v1 on v0

v1 whole, which is shorter than its diff:
```python
import functools
import math

import jax
import jax.numpy as jnp
from jax import lax
from jax.experimental import pallas as pl
from jax.experimental.pallas import tpu as pltpu
from jax.sharding import PartitionSpec as P

WIDTH = 128
HALF = WIDTH // 2
SPAN = 128
WIN = 4
ROPE_BASE = 1000000.0
YARN_FACTOR = 4.0
YARN_INITIAL = 32768.0
BETA_FAST = 32.0
BETA_SLOW = 1.0
YARN_MSCALE = 1.0 + 0.1 * math.log(4.0)
ROOT_SCALE = 1.0 / math.sqrt(WIDTH)
LOG2E = math.log2(math.e)
F32 = jnp.float32
BF16 = jnp.bfloat16
MESH = pl.DeviceIdType.MESH


def half_pi_parts():
    a = math.floor(math.pi / 2 * 2**11) / 2**11
    rest = math.pi / 2 - a
    shift = 11 - math.floor(math.log2(rest))
    b = math.floor(rest * 2.0**shift) / 2.0**shift
    return a, b, rest - b


def cos_sin(angle):
    a, b, c = half_pi_parts()
    turns = jnp.floor(angle * (2.0 / math.pi) + 0.5)
    rest = ((angle - turns * a) - turns * b) - turns * c
    quadrant = turns.astype(jnp.int32) & 3
    square = rest * rest
    sine = rest + rest * square * (
        -1.0 / 6 + square * (1.0 / 120 + square * (-1.0 / 5040 + square * (1.0 / 362880)))
    )
    cosine = 1.0 + square * (
        -0.5
        + square
        * (1.0 / 24 + square * (-1.0 / 720 + square * (1.0 / 40320 - square * (1.0 / 3628800))))
    )
    swap = (quadrant & 1) == 1
    cos_out = jnp.where(swap, sine, cosine)
    sin_out = jnp.where(swap, cosine, sine)
    cos_out = jnp.where((quadrant == 1) | (quadrant == 2), -cos_out, cos_out)
    sin_out = jnp.where(quadrant >= 2, -sin_out, sin_out)
    return cos_out, sin_out


def frequencies(shape):
    pair = lax.broadcasted_iota(jnp.int32, shape, 0).astype(F32)
    inverse = jnp.exp(-2.0 * pair / WIDTH * math.log(ROPE_BASE))
    ratio = YARN_INITIAL * inverse / (2.0 * math.pi)
    ramp = jnp.clip((ratio - BETA_SLOW) / (BETA_FAST - BETA_SLOW), 0.0, 1.0)
    return inverse * ((1.0 - ramp) / YARN_FACTOR + ramp)


def dot(a, b, a_dim, b_dim):
    return lax.dot_general(a, b, (((a_dim,), (b_dim,)), ((), ())), preferred_element_type=F32)


def kernel(
    groups,
    share,
    n_ctx,
    n_head,
    span_ref,
    q_hbm,
    k_hbm,
    v_hbm,
    g_hbm,
    o_hbm,
    lse_hbm,
    pos_hbm,
    dq_hbm,
    dk_hbm,
    dv_hbm,
    q_raw,
    k_raw,
    g_raw,
    o_raw,
    lse_raw,
    pos_all,
    q_s,
    g_s,
    lse_s,
    delta_s,
    tab_t,
    tab_n,
    kbuf,
    vbuf,
    dq_acc,
    dq_out,
    own,
    part,
    ret_send,
    ret_recv,
    dkv_out,
    load_sem,
    store_sem,
    pos_ssem,
    pos_rsem,
    fwd_ssem,
    fwd_rsem,
    ret_ssem,
    ret_rsem,
):
    me = lax.axis_index("ctx")
    my_head = lax.axis_index("head")
    left = lax.rem(me + (n_ctx - 1), n_ctx)
    right = lax.rem(me + 1, n_ctx)
    peers = [lax.rem(my_head + step, n_head) for step in range(1, n_head)]

    loads = {}

    def load(name, index, source, target):
        loads[name] = pltpu.make_async_copy(source, target, load_sem.at[index])
        loads[name].start()

    load("pos", 0, pos_hbm, pos_all.at[my_head])
    for g in range(groups):
        for half in range(2):
            load(
                ("v", g, half),
                1 + 2 * g + half,
                v_hbm.at[half * SPAN : (half + 1) * SPAN, g * WIDTH : (g + 1) * WIDTH],
                vbuf.at[0, g, half],
            )
    base = 1 + 2 * groups
    load("k", base, k_hbm, k_raw)
    load("q", base + 1, q_hbm, q_raw)
    load("g", base + 2, g_hbm, g_raw)
    load("o", base + 3, o_hbm, o_raw)
    load("lse", base + 4, lse_hbm, lse_raw)

    barrier = pltpu.get_barrier_semaphore()
    for ctx in (left, right):
        pl.semaphore_signal(barrier, inc=1, device_id=(ctx, my_head), device_id_type=MESH)
    for peer in peers:
        pl.semaphore_signal(barrier, inc=1, device_id=(me, peer), device_id_type=MESH)
    freq = frequencies((HALF, WIDTH))
    loads["pos"].wait()
    pl.semaphore_wait(barrier, 2 + len(peers))

    pos_copies = []
    for step, peer in enumerate(peers):
        copy = pltpu.make_async_remote_copy(
            src_ref=pos_all.at[my_head],
            dst_ref=pos_all.at[my_head],
            send_sem=pos_ssem.at[step],
            recv_sem=pos_rsem.at[step],
            device_id=(me, peer),
            device_id_type=MESH,
        )
        copy.start()
        pos_copies.append(copy)

    def forward(which, g, hop):
        buf = (vbuf, kbuf)[which]
        return pltpu.make_async_remote_copy(
            src_ref=buf.at[hop - 1, g],
            dst_ref=buf.at[hop, g],
            send_sem=fwd_ssem.at[which, g, hop - 1],
            recv_sem=fwd_rsem.at[which, g, hop - 1],
            device_id=(left, my_head),
            device_id_type=MESH,
        )

    def send_v(g, hop):
        forward(0, g, hop).start()

    def send_k(g, hop):
        forward(1, g, hop).start()

    def got_v(g, hop):
        forward(0, g, hop).wait_recv()

    def got_k(g, hop):
        forward(1, g, hop).wait_recv()

    for g in range(groups):
        for half in range(2):
            loads[("v", g, half)].wait()
        send_v(g, 1)

    for copy in pos_copies:
        copy.wait_recv()
    pieces = [pos_all[h].astype(F32) for h in range(n_head)]
    placed = jnp.concatenate(pieces, axis=1)
    pair = lax.broadcasted_iota(jnp.int32, (HALF, 2 * SPAN), 0)
    chosen = jnp.where(
        pair < WIDTH // 8,
        placed[0:1],
        jnp.where(pair < WIDTH // 8 + 3 * WIDTH // 16, placed[1:2], placed[2:3]),
    )
    cosine, sine = cos_sin(chosen * jnp.concatenate([freq, freq], axis=1))
    cosine = cosine * YARN_MSCALE
    sine = sine * YARN_MSCALE
    tab_t[0] = cosine
    tab_t[1] = sine
    tab_n[0] = jnp.concatenate([cosine, cosine], axis=0).T
    tab_n[1] = jnp.concatenate([-sine, sine], axis=0).T

    def rotated(block, half):
        wide = block.astype(F32)
        rows = slice(half * SPAN, (half + 1) * SPAN)
        return (wide * tab_n[0, rows] + pltpu.roll(wide, HALF, 1) * tab_n[1, rows]).astype(BF16)

    def unrotated(wide, half):
        rows = slice(half * SPAN, (half + 1) * SPAN)
        return wide * tab_n[0, rows] - pltpu.roll(wide, HALF, 1) * tab_n[1, rows]

    loads["k"].wait()
    for g in range(groups):
        for half in range(2):
            kbuf[0, g, half] = rotated(
                k_raw[half * SPAN : (half + 1) * SPAN, g * WIDTH : (g + 1) * WIDTH], half
            )
        if g == 0:
            send_k(0, 1)

    def prepare(g):
        for half in range(2):
            rows = slice(half * SPAN, (half + 1) * SPAN)
            ones = jnp.ones((8, WIDTH), BF16)
            for j in range(share):
                head = g * share + j
                cols = slice(head * WIDTH, (head + 1) * WIDTH)
                stacked = slice(j * SPAN, (j + 1) * SPAN)
                q_s[g, half, stacked] = rotated(q_raw[rows, cols], half)
                grad = g_raw[rows, cols]
                g_s[g, half, stacked] = grad
                product = grad.astype(F32) * o_raw[rows, cols].astype(F32)
                upper = product.astype(BF16)
                lower = (product - upper.astype(F32)).astype(BF16)
                delta = dot(ones, upper, 1, 1) + dot(ones, lower, 1, 1)
                delta_s[g, half, :, stacked] = delta
                lse_s[g, half, :, stacked] = jnp.broadcast_to(
                    lse_raw[head : head + 1, rows] * LOG2E, (8, SPAN)
                )

    step_cols = 2 * SPAN

    def unit(g, q_half, key, value, masked):
        value_sum = key_sum = None
        query_parts = []
        for start in range(0, share * SPAN, step_cols):
            at = slice(start, start + step_cols)
            query = q_s[g, q_half, at]
            grad = g_s[g, q_half, at]
            scores = dot(key, query, 1, 1)
            exponent = scores * (ROOT_SCALE * LOG2E) - lse_s[g, q_half, 0:1, at]
            weights = jnp.exp2(exponent)
            if masked:
                shape = (SPAN, step_cols)
                key_at = lax.broadcasted_iota(jnp.int32, shape, 0)
                query_at = lax.broadcasted_iota(jnp.int32, shape, 1) & (SPAN - 1)
                weights = jnp.where(key_at <= query_at, weights, 0.0)
            weight_grad = dot(value, grad, 1, 1)
            score_grad = weights * (weight_grad - delta_s[g, q_half, 0:1, at])
            rounded_weights = weights.astype(BF16)
            rounded_grad = score_grad.astype(BF16)
            value_part = dot(rounded_weights, grad, 1, 0)
            key_part = dot(rounded_grad, query, 1, 0)
            value_sum = value_part if value_sum is None else value_sum + value_part
            key_sum = key_part if key_sum is None else key_sum + key_part
            query_parts.append(dot(key, rounded_grad, 0, 0))
        return value_sum, key_sum, jnp.concatenate(query_parts, axis=1)

    my_span = span_ref[me]

    def own_block(g):
        k0, k1, v0, v1 = kbuf[0, g, 0], kbuf[0, g, 1], vbuf[0, g, 0], vbuf[0, g, 1]
        dv, dk, dq = unit(g, 0, k0, v0, True)
        dq_acc[g, 0] = dq
        dv_next, dk_next, dq = unit(g, 1, k0, v0, False)
        own[g, 0, 0] = dv + dv_next
        own[g, 1, 0] = dk + dk_next
        dv, dk, dq_next = unit(g, 1, k1, v1, True)
        own[g, 0, 1] = dv
        own[g, 1, 1] = dk
        dq_acc[g, 1] = dq + dq_next

    def other_block(g, hop):
        lower = span_ref[lax.rem(me + hop, n_ctx)] < my_span
        k0, k1, v0, v1 = kbuf[hop, g, 0], kbuf[hop, g, 1], vbuf[hop, g, 0], vbuf[hop, g, 1]
        dv, dk, dq = unit(g, 1, k0, v0, False)
        dq_acc[g, 1] += dq
        picked = jnp.where(lower, 0, 1)
        dv_x, dk_x, dq_x = unit(
            g, picked, jnp.where(lower, k0, k1), jnp.where(lower, v0, v1), False
        )
        dq_acc[g, 0] += jnp.where(lower, dq_x, 0.0)
        dq_acc[g, 1] += jnp.where(lower, 0.0, dq_x)
        for which, first, second in ((0, dv, dv_x), (1, dk, dk_x)):
            early = first + jnp.where(lower, second, 0.0)
            late = jnp.where(lower, 0.0, second)
            if hop == WIN - 1:
                ret_send[g, hop - 1, which, 0] = early.astype(BF16)
                ret_send[g, hop - 1, which, 1] = late.astype(BF16)
                back(which, g, hop).start()
            else:
                part[g, hop - 1, which, 0] = early
                part[g, hop - 1, which, 1] = late

    def back(which, g, hop):
        return pltpu.make_async_remote_copy(
            src_ref=ret_send.at[g, hop - 1, which],
            dst_ref=ret_recv.at[g, hop - 1, which],
            send_sem=ret_ssem.at[which, g, hop - 1],
            recv_sem=ret_rsem.at[which, g, hop - 1],
            device_id=(right, my_head),
            device_id_type=MESH,
        )

    def pass_on(g, hop):
        for which in range(2):
            back(which, g, hop + 1).wait_recv()
            ret_send[g, hop - 1, which] = (
                ret_recv[g, hop, which].astype(F32) + part[g, hop - 1, which]
            ).astype(BF16)
            back(which, g, hop).start()

    stores = []

    def store(source, target):
        copy = pltpu.make_async_copy(source, target, store_sem.at[len(stores)])
        copy.start()
        stores.append(copy)

    def finish_query(g):
        for half in range(2):
            rows = slice(half * SPAN, (half + 1) * SPAN)
            cosine = tab_t[0, :, rows] * ROOT_SCALE
            sine = tab_t[1, :, rows] * ROOT_SCALE
            for j in range(share):
                stacked = slice(j * SPAN, (j + 1) * SPAN)
                first = dq_acc[g, half, 0:HALF, stacked]
                second = dq_acc[g, half, HALF:WIDTH, stacked]
                turned = jnp.concatenate(
                    [first * cosine + second * sine, second * cosine - first * sine], axis=0
                )
                head = g * share + j
                dq_out[rows, head * WIDTH : (head + 1) * WIDTH] = turned.T.astype(BF16)
        cols = slice(g * share * WIDTH, (g + 1) * share * WIDTH)
        store(dq_out.at[:, cols], dq_hbm.at[:, cols])

    def finish_keys(g):
        cols = slice(g * WIDTH, (g + 1) * WIDTH)
        for which, target in ((0, dv_hbm), (1, dk_hbm)):
            back(which, g, 1).wait_recv()
            for half in range(2):
                rows = slice(half * SPAN, (half + 1) * SPAN)
                total = own[g, which, half] + ret_recv[g, 0, which, half].astype(F32)
                if which == 1:
                    total = unrotated(total * ROOT_SCALE, half)
                dkv_out[which, rows, cols] = total.astype(BF16)
            store(dkv_out.at[which, :, cols], target.at[:, cols])

    got_v(0, 1)
    send_v(0, 2)
    for name in ("q", "g", "o", "lse"):
        loads[name].wait()
    prepare(0)
    got_k(0, 1)
    send_k(0, 2)
    got_v(0, 2)
    send_v(0, 3)
    own_block(0)
    got_k(0, 2)
    send_k(0, 3)
    send_k(1, 1)
    other_block(0, 1)
    got_v(1, 1)
    send_v(1, 2)
    other_block(0, 2)
    got_k(1, 1)
    send_k(1, 2)
    got_v(0, 3)
    got_k(0, 3)
    other_block(0, 3)
    prepare(1)
    got_v(1, 2)
    send_v(1, 3)
    pass_on(0, 2)
    own_block(1)
    got_k(1, 2)
    send_k(1, 3)
    pass_on(0, 1)
    other_block(1, 1)
    other_block(1, 2)
    got_v(1, 3)
    got_k(1, 3)
    other_block(1, 3)
    finish_query(0)
    finish_keys(0)
    pass_on(1, 2)
    finish_query(1)
    pass_on(1, 1)
    finish_keys(1)

    for copy in pos_copies:
        copy.wait_send()
    for g in range(groups):
        for which in range(2):
            for hop in range(1, WIN):
                forward(which, g, hop).wait_send()
                back(which, g, hop).wait_send()
    for copy in stores:
        copy.wait()


def shards(query, key, value, out_grad, attn_out, log_sum_exp, positions, span_map):
    rows = query.shape[0]
    heads = query.shape[1] // WIDTH
    groups = key.shape[1] // WIDTH
    share = heads // groups
    n_ctx = lax.axis_size("ctx")
    n_head = lax.axis_size("head")
    hops = WIN - 1
    dma = pltpu.SemaphoreType.DMA
    anywhere = pl.BlockSpec(memory_space=pl.ANY)
    return pl.pallas_call(
        functools.partial(kernel, groups, share, n_ctx, n_head),
        out_shape=(
            jax.ShapeDtypeStruct((rows, heads * WIDTH), BF16),
            jax.ShapeDtypeStruct((rows, groups * WIDTH), BF16),
            jax.ShapeDtypeStruct((rows, groups * WIDTH), BF16),
        ),
        in_specs=[pl.BlockSpec(memory_space=pltpu.SMEM)] + [anywhere] * 7,
        out_specs=(anywhere,) * 3,
        scratch_shapes=[
            pltpu.VMEM((rows, heads * WIDTH), BF16),
            pltpu.VMEM((rows, groups * WIDTH), BF16),
            pltpu.VMEM((rows, heads * WIDTH), BF16),
            pltpu.VMEM((rows, heads * WIDTH), BF16),
            pltpu.VMEM((heads, rows), F32),
            pltpu.VMEM((n_head,) + positions.shape, jnp.int32),
            pltpu.VMEM((groups, 2, share * SPAN, WIDTH), BF16),
            pltpu.VMEM((groups, 2, share * SPAN, WIDTH), BF16),
            pltpu.VMEM((groups, 2, 8, share * SPAN), F32),
            pltpu.VMEM((groups, 2, 8, share * SPAN), F32),
            pltpu.VMEM((2, HALF, rows), F32),
            pltpu.VMEM((2, rows, WIDTH), F32),
            pltpu.VMEM((WIN, groups, 2, SPAN, WIDTH), BF16),
            pltpu.VMEM((WIN, groups, 2, SPAN, WIDTH), BF16),
            pltpu.VMEM((groups, 2, WIDTH, share * SPAN), F32),
            pltpu.VMEM((rows, heads * WIDTH), BF16),
            pltpu.VMEM((groups, 2, 2, SPAN, WIDTH), F32),
            pltpu.VMEM((groups, hops - 1, 2, 2, SPAN, WIDTH), F32),
            pltpu.VMEM((groups, hops, 2, 2, SPAN, WIDTH), BF16),
            pltpu.VMEM((groups, hops, 2, 2, SPAN, WIDTH), BF16),
            pltpu.VMEM((2, rows, groups * WIDTH), BF16),
            dma((6 + 2 * groups,)),
            dma((3 * groups,)),
            dma((n_head - 1,)),
            dma((n_head - 1,)),
            dma((2, groups, hops)),
            dma((2, groups, hops)),
            dma((2, groups, hops)),
            dma((2, groups, hops)),
        ],
        compiler_params=pltpu.CompilerParams(
            collective_id=0, has_side_effects=True, vmem_limit_bytes=40 * 2**20
        ),
        cost_estimate=pl.CostEstimate(
            flops=10 * heads * 9 * SPAN * SPAN * WIDTH,
            bytes_accessed=8 * rows * heads * WIDTH + 8 * rows * groups * WIDTH,
            transcendentals=heads * 9 * SPAN * SPAN,
        ),
    )(span_map, query, key, value, out_grad, attn_out, log_sum_exp, positions)


def solution(mesh):
    placed = (
        P("ctx", "head"),
        P("ctx", "head"),
        P("ctx", "head"),
        P("ctx", "head"),
        P("ctx", "head"),
        P("head", "ctx"),
        P(None, ("ctx", "head")),
        P(),
    )
    return jax.shard_map(
        shards,
        mesh=mesh,
        in_specs=placed,
        out_specs=(P("ctx", "head"), P("ctx", "head"), P("ctx", "head")),
        check_vma=False,
    )
```

time: 256 us -> 67.5 us (0.26)
  the two profiles are of different devices: /device:TPU:2 before, /device:TPU:64 now
where the time goes in v1:
time: 67.5 us; the launch traced here: 67.2 us
  Pallas kernels  57.5 us (85%)
  local copies, waits for them, and re-layouts  9.06 us (13%)
    pallas_call x1, Pallas kernels, shards(): pl.pallas_call(functools.partial(kernel, groups, share, n_ctx, n_head), o...  57.5 us
    unnamed x19, local copies, waits for them, and re-layouts  9.06 us

profile of v1, /device:TPU:64, one launch (start us, length us, event | category | flops | bytes accessed | tf_op | source)
XLA Modules:
  0.0 67.2 jit_solution(14948186468348250777)
XLA Ops:
  0.6 0.0 copy-start
  0.6 1.0 %copy-done = bf16[256,1024]{1,0:T(8,128)(2,1)S(1)} copy-done((bf16[256,1024]{1,0:T(8,128)(2,1)S(1)}, bf16[256,1024]{1,0:T(8,128)(2,1)}, u32[]{:S(2)}) %copy-start) | copy-done | bytes 524312
  1.7 0.0 copy-start.1
  1.7 1.0 %copy-done.1 = bf16[256,1024]{1,0:T(8,128)(2,1)S(1)} copy-done((bf16[256,1024]{1,0:T(8,128)(2,1)S(1)}, bf16[256,1024]{1,0:T(8,128)(2,1)}, u32[]{:S(2)}) %copy-start.1) | copy-done | bytes 524312
  2.7 0.0 copy-start.2
  2.7 1.0 %copy-done.2 = bf16[256,1024]{1,0:T(8,128)(2,1)S(1)} copy-done((bf16[256,1024]{1,0:T(8,128)(2,1)S(1)}, bf16[256,1024]{1,0:T(8,128)(2,1)}, u32[]{:S(2)}) %copy-start.2) | copy-done | bytes 524312
  3.8 0.0 copy-start.3
  3.8 0.9 %copy-done.3 = bf16[256,256]{1,0:T(8,128)(2,1)S(1)} copy-done((bf16[256,256]{1,0:T(8,128)(2,1)S(1)}, bf16[256,256]{1,0:T(8,128)(2,1)}, u32[]{:S(2)}) %copy-start.3) | copy-done | bytes 131096
  4.7 0.0 copy-start.4
  4.7 0.9 %copy-done.4 = bf16[256,256]{1,0:T(8,128)(2,1)S(1)} copy-done((bf16[256,256]{1,0:T(8,128)(2,1)S(1)}, bf16[256,256]{1,0:T(8,128)(2,1)}, u32[]{:S(2)}) %copy-start.4) | copy-done | bytes 131096
  5.6 0.0 copy-start.5
  5.6 0.7 %copy-done.5 = f32[8,256]{1,0:T(8,128)S(1)} copy-done((f32[8,256]{1,0:T(8,128)S(1)}, f32[8,256]{1,0:T(8,128)}, u32[]{:S(2)}) %copy-start.5) | copy-done | bytes 8216
  6.3 0.0 copy-start.6
  6.3 0.7 %copy-done.6 = s32[3,64]{1,0:T(4,128)S(1)} copy-done((s32[3,64]{1,0:T(4,128)S(1)}, s32[3,64]{1,0:T(4,128)}, u32[]{:S(2)}) %copy-start.6) | copy-done | bytes 792
  6.9 0.0 copy-start.7
  7.0 0.7 copy-done.7
  7.6 57.5 %shard_map.103 = (bf16[256,1024]{1,0:T(8,128)(2,1)S(1)}, bf16[256,256]{1,0:T(8,128)(2,1)S(1)}, bf16[256,256]{1,0:T(8,128)(2,1)S(1)}) custom-call(s32[64]{0:T(128)S(1)} %copy-done.7, bf16[256,1024]{1,0:T(8,128)(2,1)S(1)} %copy-done, bf16[256,256]{1,0:T(8,128)(2,1)S(1)} %copy-done.3, bf16[256,256]{1,0:T(8,128)(2,1)S(1)} %copy-done.4, ...), custom_call_target="tpu_custom_call" | custom-call | flops 1509949440 | bytes 2621440 | tf_op jit(solution)/shard_map/pallas_call | solution.py:431
  65.1 0.8 %copy.14 = bf16[256,1024]{1,0:T(8,128)(2,1)} copy(bf16[256,1024]{1,0:T(8,128)(2,1)S(1)} %get-tuple-element.6) | data formatting | bytes 1048576
  65.9 0.7 copy.15
  66.5 0.7 copy.16
Async XLA Ops:
  0.6 1.0 %copy-start = (bf16[256,1024]{1,0:T(8,128)(2,1)S(1)}, bf16[256,1024]{1,0:T(8,128)(2,1)}, u32[]{:S(2)}) copy-start(bf16[256,1024]{1,0:T(8,128)(2,1)} %q_hbm.1) | copy-start | bytes 1572868
  1.7 1.0 %copy-start.1 = (bf16[256,1024]{1,0:T(8,128)(2,1)S(1)}, bf16[256,1024]{1,0:T(8,128)(2,1)}, u32[]{:S(2)}) copy-start(bf16[256,1024]{1,0:T(8,128)(2,1)} %g_hbm.1) | copy-start | bytes 1572868
  2.7 1.0 %copy-start.2 = (bf16[256,1024]{1,0:T(8,128)(2,1)S(1)}, bf16[256,1024]{1,0:T(8,128)(2,1)}, u32[]{:S(2)}) copy-start(bf16[256,1024]{1,0:T(8,128)(2,1)} %o_hbm.1) | copy-start | bytes 1572868
  3.8 0.9 %copy-start.3 = (bf16[256,256]{1,0:T(8,128)(2,1)S(1)}, bf16[256,256]{1,0:T(8,128)(2,1)}, u32[]{:S(2)}) copy-start(bf16[256,256]{1,0:T(8,128)(2,1)} %k_hbm.1) | copy-start | bytes 393220
  4.7 0.9 %copy-start.4 = (bf16[256,256]{1,0:T(8,128)(2,1)S(1)}, bf16[256,256]{1,0:T(8,128)(2,1)}, u32[]{:S(2)}) copy-start(bf16[256,256]{1,0:T(8,128)(2,1)} %v_hbm.1) | copy-start | bytes 393220
  5.6 0.7 %copy-start.5 = (f32[8,256]{1,0:T(8,128)S(1)}, f32[8,256]{1,0:T(8,128)}, u32[]{:S(2)}) copy-start(f32[8,256]{1,0:T(8,128)} %lse_hbm.1) | copy-start | bytes 24580
  6.3 0.7 %copy-start.6 = (s32[3,64]{1,0:T(4,128)S(1)}, s32[3,64]{1,0:T(4,128)}, u32[]{:S(2)}) copy-start(s32[3,64]{1,0:T(4,128)} %pos_hbm.1) | copy-start | bytes 2308
  6.9 0.7 copy-start.7

commit v2 on v1

--- a/solution.py
+++ b/solution.py
@@ -23,6 +23,47 @@
 F32 = jnp.float32
 BF16 = jnp.bfloat16
 MESH = pl.DeviceIdType.MESH
+DIRECT = ()
+ORDER = (
+    ("prepare", 0),
+    ("pass", 0, 1),
+    ("pass", 2, 1),
+    ("pass", 0, 2),
+    ("pass", 1, 1),
+    ("pass", 2, 2),
+    ("pass", 3, 1),
+    ("block", 0, 2),
+    ("prepare", 1),
+    ("block", 0, 3),
+    ("pass", 1, 2),
+    ("block", 2, 2),
+    ("block", 2, 3),
+    ("pass", 3, 2),
+    ("return", 0, 2),
+    ("block", 3, 1),
+    ("block", 1, 3),
+    ("block", 0, 1),
+    ("return", 2, 2),
+    ("block", 3, 3),
+    ("return", 0, 1),
+    ("block", 1, 2),
+    ("block", 3, 2),
+    ("return", 1, 2),
+    ("block", 2, 1),
+    ("own", 0),
+    ("return", 3, 2),
+    ("return", 2, 1),
+    ("block", 1, 1),
+    ("return", 1, 1),
+    ("own", 1),
+    ("return", 3, 1),
+    ("keys", 0),
+    ("query", 1),
+    ("keys", 1),
+    ("keys", 2),
+    ("query", 0),
+    ("keys", 3),
+)
 
 
 def half_pi_parts():
@@ -95,8 +136,7 @@
     delta_s,
     tab_t,
     tab_n,
-    kbuf,
-    vbuf,
+    kv,
     dq_acc,
     dq_out,
     own,
@@ -117,6 +157,7 @@
     my_head = lax.axis_index("head")
     left = lax.rem(me + (n_ctx - 1), n_ctx)
     right = lax.rem(me + 1, n_ctx)
+    far = range(2, WIN) if DIRECT else ()
     peers = [lax.rem(my_head + step, n_head) for step in range(1, n_head)]
 
     loads = {}
@@ -126,15 +167,16 @@
         loads[name].start()
 
     load("pos", 0, pos_hbm, pos_all.at[my_head])
-    for g in range(groups):
-        for half in range(2):
-            load(
-                ("v", g, half),
-                1 + 2 * g + half,
-                v_hbm.at[half * SPAN : (half + 1) * SPAN, g * WIDTH : (g + 1) * WIDTH],
-                vbuf.at[0, g, half],
-            )
-    base = 1 + 2 * groups
+    chunks = 2 * groups
+    for chunk in range(chunks):
+        g, half = chunk // 2, chunk % 2
+        load(
+            ("v", chunk),
+            1 + chunk,
+            v_hbm.at[half * SPAN : (half + 1) * SPAN, g * WIDTH : (g + 1) * WIDTH],
+            kv.at[0, chunk, 0],
+        )
+    base = 1 + chunks
     load("k", base, k_hbm, k_raw)
     load("q", base + 1, q_hbm, q_raw)
     load("g", base + 2, g_hbm, g_raw)
@@ -142,13 +184,13 @@
     load("lse", base + 4, lse_hbm, lse_raw)
 
     barrier = pltpu.get_barrier_semaphore()
-    for ctx in (left, right):
+    for ctx in [left, right] + [lax.rem(me + (n_ctx - hop), n_ctx) for hop in far]:
         pl.semaphore_signal(barrier, inc=1, device_id=(ctx, my_head), device_id_type=MESH)
     for peer in peers:
         pl.semaphore_signal(barrier, inc=1, device_id=(me, peer), device_id_type=MESH)
     freq = frequencies((HALF, WIDTH))
     loads["pos"].wait()
-    pl.semaphore_wait(barrier, 2 + len(peers))
+    pl.semaphore_wait(barrier, 2 + len(far) + len(peers))
 
     pos_copies = []
     for step, peer in enumerate(peers):
@@ -163,33 +205,19 @@
         copy.start()
         pos_copies.append(copy)
 
-    def forward(which, g, hop):
-        buf = (vbuf, kbuf)[which]
+    def forward(which, chunk, hop):
         return pltpu.make_async_remote_copy(
-            src_ref=buf.at[hop - 1, g],
-            dst_ref=buf.at[hop, g],
-            send_sem=fwd_ssem.at[which, g, hop - 1],
-            recv_sem=fwd_rsem.at[which, g, hop - 1],
+            src_ref=kv.at[hop - 1, chunk, which],
+            dst_ref=kv.at[hop, chunk, which],
+            send_sem=fwd_ssem.at[which, chunk, hop - 1],
+            recv_sem=fwd_rsem.at[which, chunk, hop - 1],
             device_id=(left, my_head),
             device_id_type=MESH,
         )
 
-    def send_v(g, hop):
-        forward(0, g, hop).start()
-
-    def send_k(g, hop):
-        forward(1, g, hop).start()
-
-    def got_v(g, hop):
-        forward(0, g, hop).wait_recv()
-
-    def got_k(g, hop):
-        forward(1, g, hop).wait_recv()
-
-    for g in range(groups):
-        for half in range(2):
-            loads[("v", g, half)].wait()
-        send_v(g, 1)
+    for chunk in range(chunks):
+        loads[("v", chunk)].wait()
+        forward(0, chunk, 1).start()
 
     for copy in pos_copies:
         copy.wait_recv()
@@ -219,13 +247,12 @@
         return wide * tab_n[0, rows] - pltpu.roll(wide, HALF, 1) * tab_n[1, rows]
 
     loads["k"].wait()
-    for g in range(groups):
-        for half in range(2):
-            kbuf[0, g, half] = rotated(
-                k_raw[half * SPAN : (half + 1) * SPAN, g * WIDTH : (g + 1) * WIDTH], half
-            )
-        if g == 0:
-            send_k(0, 1)
+    for chunk in range(chunks):
+        g, half = chunk // 2, chunk % 2
+        kv[0, chunk, 1] = rotated(
+            k_raw[half * SPAN : (half + 1) * SPAN, g * WIDTH : (g + 1) * WIDTH], half
+        )
+        forward(1, chunk, 1).start()
 
     def prepare(g):
         for half in range(2):
@@ -249,17 +276,18 @@
 
     step_cols = 2 * SPAN
 
-    def unit(g, q_half, key, value, masked):
+    def unit(g, q_half, key, value, causal=False, visible=None):
         value_sum = key_sum = None
         query_parts = []
         for start in range(0, share * SPAN, step_cols):
             at = slice(start, start + step_cols)
             query = q_s[g, q_half, at]
             grad = g_s[g, q_half, at]
-            scores = dot(key, query, 1, 1)
-            exponent = scores * (ROOT_SCALE * LOG2E) - lse_s[g, q_half, 0:1, at]
-            weights = jnp.exp2(exponent)
-            if masked:
+            norm = lse_s[g, q_half, 0:1, at]
+            if visible is not None:
+                norm = jnp.where(visible, norm, 1e30)
+            weights = jnp.exp2(dot(key, query, 1, 1) * (ROOT_SCALE * LOG2E) - norm)
+            if causal:
                 shape = (SPAN, step_cols)
                 key_at = lax.broadcasted_iota(jnp.int32, shape, 0)
                 query_at = lax.broadcasted_iota(jnp.int32, shape, 1) & (SPAN - 1)
@@ -277,57 +305,69 @@
 
     my_span = span_ref[me]
 
+    begun = set()
+
+    def add_query(g, half, value):
+        if (g, half) in begun:
+            value = dq_acc[g, half] + value
+        begun.add((g, half))
+        dq_acc[g, half] = value
+
     def own_block(g):
-        k0, k1, v0, v1 = kbuf[0, g, 0], kbuf[0, g, 1], vbuf[0, g, 0], vbuf[0, g, 1]
-        dv, dk, dq = unit(g, 0, k0, v0, True)
-        dq_acc[g, 0] = dq
-        dv_next, dk_next, dq = unit(g, 1, k0, v0, False)
-        own[g, 0, 0] = dv + dv_next
-        own[g, 1, 0] = dk + dk_next
-        dv, dk, dq_next = unit(g, 1, k1, v1, True)
-        own[g, 0, 1] = dv
-        own[g, 1, 1] = dk
-        dq_acc[g, 1] = dq + dq_next
-
-    def other_block(g, hop):
+        early, late = 2 * g, 2 * g + 1
+        dv, dk, dq = unit(g, 0, kv[0, early, 1], kv[0, early, 0], causal=True)
+        add_query(g, 0, dq)
+        dv_next, dk_next, dq = unit(g, 1, kv[0, early, 1], kv[0, early, 0])
+        own[early, 0] = dv + dv_next
+        own[early, 1] = dk + dk_next
+        dv, dk, dq_next = unit(g, 1, kv[0, late, 1], kv[0, late, 0], causal=True)
+        own[late, 0] = dv
+        own[late, 1] = dk
+        add_query(g, 1, dq + dq_next)
+
+    def got(chunk, hop):
+        for which in range(2):
+            forward(which, chunk, hop).wait_recv()
+
+    def other_block(chunk, hop):
+        g, half = chunk // 2, chunk % 2
         lower = span_ref[lax.rem(me + hop, n_ctx)] < my_span
-        k0, k1, v0, v1 = kbuf[hop, g, 0], kbuf[hop, g, 1], vbuf[hop, g, 0], vbuf[hop, g, 1]
-        dv, dk, dq = unit(g, 1, k0, v0, False)
-        dq_acc[g, 1] += dq
-        picked = jnp.where(lower, 0, 1)
-        dv_x, dk_x, dq_x = unit(
-            g, picked, jnp.where(lower, k0, k1), jnp.where(lower, v0, v1), False
-        )
-        dq_acc[g, 0] += jnp.where(lower, dq_x, 0.0)
-        dq_acc[g, 1] += jnp.where(lower, 0.0, dq_x)
-        for which, first, second in ((0, dv, dv_x), (1, dk, dk_x)):
-            early = first + jnp.where(lower, second, 0.0)
-            late = jnp.where(lower, 0.0, second)
-            if hop == WIN - 1:
-                ret_send[g, hop - 1, which, 0] = early.astype(BF16)
-                ret_send[g, hop - 1, which, 1] = late.astype(BF16)
-                back(which, g, hop).start()
+        key, value = kv[hop, chunk, 1], kv[hop, chunk, 0]
+        if half == 0:
+            dv, dk, dq = unit(g, 1, key, value)
+            add_query(g, 1, dq)
+            dv_next, dk_next, dq = unit(g, 0, key, value, visible=lower)
+            add_query(g, 0, dq)
+            sums = (dv + dv_next, dk + dk_next)
+        else:
+            dv, dk, dq = unit(g, 1, key, value, visible=jnp.logical_not(lower))
+            add_query(g, 1, dq)
+            sums = (dv, dk)
+        for which in range(2):
+            if hop == WIN - 1 or chunk in DIRECT:
+                ret_send[chunk, hop - 1, which] = sums[which].astype(BF16)
+                back(which, chunk, hop).start()
             else:
-                part[g, hop - 1, which, 0] = early
-                part[g, hop - 1, which, 1] = late
-
-    def back(which, g, hop):
+                part[chunk, hop - 1, which] = sums[which]
+
+    def back(which, chunk, hop):
+        target = lax.rem(me + hop, n_ctx) if chunk in DIRECT else right
         return pltpu.make_async_remote_copy(
-            src_ref=ret_send.at[g, hop - 1, which],
-            dst_ref=ret_recv.at[g, hop - 1, which],
-            send_sem=ret_ssem.at[which, g, hop - 1],
-            recv_sem=ret_rsem.at[which, g, hop - 1],
-            device_id=(right, my_head),
+            src_ref=ret_send.at[chunk, hop - 1, which],
+            dst_ref=ret_recv.at[chunk, hop - 1, which],
+            send_sem=ret_ssem.at[which, chunk, hop - 1],
+            recv_sem=ret_rsem.at[which, chunk, hop - 1],
+            device_id=(target, my_head),
             device_id_type=MESH,
         )
 
-    def pass_on(g, hop):
+    def pass_on(chunk, hop):
         for which in range(2):
-            back(which, g, hop + 1).wait_recv()
-            ret_send[g, hop - 1, which] = (
-                ret_recv[g, hop, which].astype(F32) + part[g, hop - 1, which]
+            back(which, chunk, hop + 1).wait_recv()
+            ret_send[chunk, hop - 1, which] = (
+                ret_recv[chunk, hop, which].astype(F32) + part[chunk, hop - 1, which]
             ).astype(BF16)
-            back(which, g, hop).start()
+            back(which, chunk, hop).start()
 
     stores = []
 
@@ -353,67 +393,51 @@
         cols = slice(g * share * WIDTH, (g + 1) * share * WIDTH)
         store(dq_out.at[:, cols], dq_hbm.at[:, cols])
 
-    def finish_keys(g):
+    def finish_keys(chunk):
+        g, half = chunk // 2, chunk % 2
+        rows = slice(half * SPAN, (half + 1) * SPAN)
         cols = slice(g * WIDTH, (g + 1) * WIDTH)
         for which, target in ((0, dv_hbm), (1, dk_hbm)):
-            back(which, g, 1).wait_recv()
-            for half in range(2):
-                rows = slice(half * SPAN, (half + 1) * SPAN)
-                total = own[g, which, half] + ret_recv[g, 0, which, half].astype(F32)
-                if which == 1:
-                    total = unrotated(total * ROOT_SCALE, half)
-                dkv_out[which, rows, cols] = total.astype(BF16)
-            store(dkv_out.at[which, :, cols], target.at[:, cols])
-
-    got_v(0, 1)
-    send_v(0, 2)
+            total = own[chunk, which]
+            for hop in range(WIN - 1 if chunk in DIRECT else 1, 0, -1):
+                back(which, chunk, hop).wait_recv()
+                total = total + ret_recv[chunk, hop - 1, which].astype(F32)
+            if which == 1:
+                total = unrotated(total * ROOT_SCALE, half)
+            dkv_out[which, rows, cols] = total.astype(BF16)
+            store(dkv_out.at[which, rows, cols], target.at[rows, cols])
+
     for name in ("q", "g", "o", "lse"):
         loads[name].wait()
-    prepare(0)
-    got_k(0, 1)
-    send_k(0, 2)
-    got_v(0, 2)
-    send_v(0, 3)
-    own_block(0)
-    got_k(0, 2)
-    send_k(0, 3)
-    send_k(1, 1)
-    other_block(0, 1)
-    got_v(1, 1)
-    send_v(1, 2)
-    other_block(0, 2)
-    got_k(1, 1)
-    send_k(1, 2)
-    got_v(0, 3)
-    got_k(0, 3)
-    other_block(0, 3)
-    prepare(1)
-    got_v(1, 2)
-    send_v(1, 3)
-    pass_on(0, 2)
-    own_block(1)
-    got_k(1, 2)
-    send_k(1, 3)
-    pass_on(0, 1)
-    other_block(1, 1)
-    other_block(1, 2)
-    got_v(1, 3)
-    got_k(1, 3)
-    other_block(1, 3)
-    finish_query(0)
-    finish_keys(0)
-    pass_on(1, 2)
-    finish_query(1)
-    pass_on(1, 1)
-    finish_keys(1)
+    for what, *at in ORDER:
+        if what == "prepare":
+            prepare(*at)
+        elif what == "own":
+            own_block(*at)
+        elif what == "pass":
+            chunk, hop = at
+            got(chunk, hop)
+            for which in range(2):
+                forward(which, chunk, hop + 1).start()
+        elif what == "block":
+            chunk, hop = at
+            if hop == WIN - 1:
+                got(chunk, hop)
+            other_block(chunk, hop)
+        elif what == "return":
+            pass_on(*at)
+        elif what == "query":
+            finish_query(*at)
+        else:
+            finish_keys(*at)
 
     for copy in pos_copies:
         copy.wait_send()
-    for g in range(groups):
+    for chunk in range(chunks):
         for which in range(2):
             for hop in range(1, WIN):
-                forward(which, g, hop).wait_send()
-                back(which, g, hop).wait_send()
+                forward(which, chunk, hop).wait_send()
+                back(which, chunk, hop).wait_send()
     for copy in stores:
         copy.wait()
 
@@ -426,6 +450,7 @@
     n_ctx = lax.axis_size("ctx")
     n_head = lax.axis_size("head")
     hops = WIN - 1
+    chunks = 2 * groups
     dma = pltpu.SemaphoreType.DMA
     anywhere = pl.BlockSpec(memory_space=pl.ANY)
     return pl.pallas_call(
@@ -450,23 +475,22 @@
             pltpu.VMEM((groups, 2, 8, share * SPAN), F32),
             pltpu.VMEM((2, HALF, rows), F32),
             pltpu.VMEM((2, rows, WIDTH), F32),
-            pltpu.VMEM((WIN, groups, 2, SPAN, WIDTH), BF16),
-            pltpu.VMEM((WIN, groups, 2, SPAN, WIDTH), BF16),
+            pltpu.VMEM((WIN, chunks, 2, SPAN, WIDTH), BF16),
             pltpu.VMEM((groups, 2, WIDTH, share * SPAN), F32),
             pltpu.VMEM((rows, heads * WIDTH), BF16),
-            pltpu.VMEM((groups, 2, 2, SPAN, WIDTH), F32),
-            pltpu.VMEM((groups, hops - 1, 2, 2, SPAN, WIDTH), F32),
-            pltpu.VMEM((groups, hops, 2, 2, SPAN, WIDTH), BF16),
-            pltpu.VMEM((groups, hops, 2, 2, SPAN, WIDTH), BF16),
+            pltpu.VMEM((chunks, 2, SPAN, WIDTH), F32),
+            pltpu.VMEM((chunks, hops - 1, 2, SPAN, WIDTH), F32),
+            pltpu.VMEM((chunks, hops, 2, SPAN, WIDTH), BF16),
+            pltpu.VMEM((chunks, hops, 2, SPAN, WIDTH), BF16),
             pltpu.VMEM((2, rows, groups * WIDTH), BF16),
-            dma((6 + 2 * groups,)),
-            dma((3 * groups,)),
+            dma((6 + chunks,)),
+            dma((groups + 2 * chunks,)),
             dma((n_head - 1,)),
             dma((n_head - 1,)),
-            dma((2, groups, hops)),
-            dma((2, groups, hops)),
-            dma((2, groups, hops)),
-            dma((2, groups, hops)),
+            dma((2, chunks, hops)),
+            dma((2, chunks, hops)),
+            dma((2, chunks, hops)),
+            dma((2, chunks, hops)),
         ],
         compiler_params=pltpu.CompilerParams(
             collective_id=0, has_side_effects=True, vmem_limit_bytes=40 * 2**20
@@ -476,7 +500,14 @@
             bytes_accessed=8 * rows * heads * WIDTH + 8 * rows * groups * WIDTH,
             transcendentals=heads * 9 * SPAN * SPAN,
         ),
-    )(span_map, query, key, value, out_grad, attn_out, log_sum_exp, positions)
+    )(
+        *(
+            pltpu.with_memory_space_constraint(x, pltpu.HBM)
+            for x in (
+                span_map, query, key, value, out_grad, attn_out, log_sum_exp, positions
+            )
+        ),
+    )
 
 
 def solution(mesh):

time: 67.5 us -> 55.2 us (0.82)
  the two profiles are of different devices: /device:TPU:64 before, /device:TPU:2 now
where the time goes in v2:
time: 55.2 us; the launch traced here: 55.1 us
  Pallas kernels  52.3 us (95%)
  local copies, waits for them, and re-layouts  2.11 us (4%)
  between operations  0.64 us (1%)
    pallas_call x1, Pallas kernels, shards(): pl.pallas_call(functools.partial(kernel, groups, share, n_ctx, n_head), o...  52.3 us
    unnamed x3, local copies, waits for them, and re-layouts  2.11 us

profile of v2, /device:TPU:2, one launch (start us, length us, event | category | flops | bytes accessed | tf_op | source)
XLA Modules:
  0.0 55.1 jit_solution(7451386588105699656)
XLA Ops:
  0.6 52.3 %shard_map.103 = (bf16[256,1024]{1,0:T(8,128)(2,1)S(1)}, bf16[256,256]{1,0:T(8,128)(2,1)S(1)}, bf16[256,256]{1,0:T(8,128)(2,1)S(1)}) custom-call(s32[64]{0:T(128)} %span_ref.1, bf16[256,1024]{1,0:T(8,128)(2,1)} %q_hbm.1, bf16[256,256]{1,0:T(8,128)(2,1)} %k_hbm.1, bf16[256,256]{1,0:T(8,128)(2,1)} %v_hbm.1, bf16[256,1024]{1,0:T(8,128)(2,1)} %g_hbm.1, ...), custom_call_target="tpu_custom_call" | custom-call | flops 1509949440 | bytes 2621440 | tf_op jit(solution)/shard_map/pallas_call | solution.py:456
  53.0 0.8 %copy.14 = bf16[256,1024]{1,0:T(8,128)(2,1)} copy(bf16[256,1024]{1,0:T(8,128)(2,1)S(1)} %get-tuple-element.6) | data formatting | bytes 1048576
  53.8 0.7 %copy.15 = bf16[256,256]{1,0:T(8,128)(2,1)} copy(bf16[256,256]{1,0:T(8,128)(2,1)S(1)} %get-tuple-element.7) | data formatting | bytes 262144
  54.4 0.7 %copy.16 = bf16[256,256]{1,0:T(8,128)(2,1)} copy(bf16[256,256]{1,0:T(8,128)(2,1)S(1)} %get-tuple-element.8) | data formatting | bytes 262144

commit v3 on v2

--- a/solution.py
+++ b/solution.py
@@ -23,46 +23,39 @@
 F32 = jnp.float32
 BF16 = jnp.bfloat16
 MESH = pl.DeviceIdType.MESH
-DIRECT = ()
 ORDER = (
+    ("prepare", 1),
     ("prepare", 0),
+    ("own", 0),
     ("pass", 0, 1),
     ("pass", 2, 1),
+    ("pass", 1, 1),
+    ("block", 2, 1),
     ("pass", 0, 2),
-    ("pass", 1, 1),
+    ("block", 0, 2),
+    ("pass", 3, 1),
+    ("block", 3, 1),
+    ("block", 0, 1),
     ("pass", 2, 2),
-    ("pass", 3, 1),
-    ("block", 0, 2),
-    ("prepare", 1),
+    ("block", 1, 2),
     ("block", 0, 3),
-    ("pass", 1, 2),
+    ("block", 3, 2),
+    ("block", 2, 3),
     ("block", 2, 2),
-    ("block", 2, 3),
-    ("pass", 3, 2),
     ("return", 0, 2),
-    ("block", 3, 1),
-    ("block", 1, 3),
-    ("block", 0, 1),
-    ("return", 2, 2),
-    ("block", 3, 3),
-    ("return", 0, 1),
-    ("block", 1, 2),
-    ("block", 3, 2),
-    ("return", 1, 2),
-    ("block", 2, 1),
-    ("own", 0),
-    ("return", 3, 2),
-    ("return", 2, 1),
     ("block", 1, 1),
     ("return", 1, 1),
+    ("return", 2, 2),
+    ("return", 0, 1),
     ("own", 1),
     ("return", 3, 1),
+    ("keys", 1),
+    ("query", 1),
+    ("query", 0),
+    ("return", 2, 1),
     ("keys", 0),
-    ("query", 1),
-    ("keys", 1),
+    ("keys", 3),
     ("keys", 2),
-    ("query", 0),
-    ("keys", 3),
 )
 
 
@@ -102,6 +95,10 @@
     ratio = YARN_INITIAL * inverse / (2.0 * math.pi)
     ramp = jnp.clip((ratio - BETA_SLOW) / (BETA_FAST - BETA_SLOW), 0.0, 1.0)
     return inverse * ((1.0 - ramp) / YARN_FACTOR + ramp)
+
+
+def last_hop(chunk):
+    return WIN - 1 - chunk % 2
 
 
 def dot(a, b, a_dim, b_dim):
@@ -132,11 +129,15 @@
     pos_all,
     q_s,
     g_s,
-    lse_s,
-    delta_s,
+    stat_s,
     tab_t,
     tab_n,
     kv,
+    far_q,
+    far_g,
+    far_stat,
+    far_dq_send,
+    far_dq_recv,
     dq_acc,
     dq_out,
     own,
@@ -152,12 +153,13 @@
     fwd_rsem,
     ret_ssem,
     ret_rsem,
+    far_ssem,
+    far_rsem,
 ):
     me = lax.axis_index("ctx")
     my_head = lax.axis_index("head")
     left = lax.rem(me + (n_ctx - 1), n_ctx)
     right = lax.rem(me + 1, n_ctx)
-    far = range(2, WIN) if DIRECT else ()
     peers = [lax.rem(my_head + step, n_head) for step in range(1, n_head)]
 
     loads = {}
@@ -184,13 +186,32 @@
     load("lse", base + 4, lse_hbm, lse_raw)
 
     barrier = pltpu.get_barrier_semaphore()
-    for ctx in [left, right] + [lax.rem(me + (n_ctx - hop), n_ctx) for hop in far]:
+    for ctx in (left, right):
         pl.semaphore_signal(barrier, inc=1, device_id=(ctx, my_head), device_id_type=MESH)
     for peer in peers:
         pl.semaphore_signal(barrier, inc=1, device_id=(me, peer), device_id_type=MESH)
     freq = frequencies((HALF, WIDTH))
+    for name in ("g", "o", "lse"):
+        loads[name].wait()
+    for g in range(groups):
+        for half in range(2):
+            rows = slice(half * SPAN, (half + 1) * SPAN)
+            ones = jnp.ones((8, WIDTH), BF16)
+            for j in range(share):
+                head = g * share + j
+                cols = slice(head * WIDTH, (head + 1) * WIDTH)
+                stacked = slice(j * SPAN, (j + 1) * SPAN)
+                grad = g_raw[rows, cols]
+                g_s[g, half, stacked] = grad
+                product = grad.astype(F32) * o_raw[rows, cols].astype(F32)
+                upper = product.astype(BF16)
+                lower = (product - upper.astype(F32)).astype(BF16)
+                delta = dot(ones, upper, 1, 1) + dot(ones, lower, 1, 1)
+                norm = lse_raw[head : head + 1, rows] * LOG2E
+                first = lax.broadcasted_iota(jnp.int32, (8, SPAN), 0) == 0
+                stat_s[g, half, :, stacked] = jnp.where(first, norm, delta)
     loads["pos"].wait()
-    pl.semaphore_wait(barrier, 2 + len(far) + len(peers))
+    pl.semaphore_wait(barrier, 2 + len(peers))
 
     pos_copies = []
     for step, peer in enumerate(peers):
@@ -215,9 +236,28 @@
             device_id_type=MESH,
         )
 
+    def move(g, what):
+        source, target, place = (
+            (q_s.at[g, 1], far_q.at[g], right),
+            (g_s.at[g, 1], far_g.at[g], right),
+            (stat_s.at[g, 1], far_stat.at[g], right),
+            (far_dq_send.at[g], far_dq_recv.at[g], left),
+        )[what]
+        return pltpu.make_async_remote_copy(
+            src_ref=source,
+            dst_ref=target,
+            send_sem=far_ssem.at[g, what],
+            recv_sem=far_rsem.at[g, what],
+            device_id=(place, my_head),
+            device_id_type=MESH,
+        )
+
     for chunk in range(chunks):
         loads[("v", chunk)].wait()
         forward(0, chunk, 1).start()
+    for g in range(groups):
+        move(g, 1).start()
+        move(g, 2).start()
 
     for copy in pos_copies:
         copy.wait_recv()
@@ -255,35 +295,26 @@
         forward(1, chunk, 1).start()
 
     def prepare(g):
-        for half in range(2):
+        for half in (1, 0):
             rows = slice(half * SPAN, (half + 1) * SPAN)
-            ones = jnp.ones((8, WIDTH), BF16)
             for j in range(share):
                 head = g * share + j
                 cols = slice(head * WIDTH, (head + 1) * WIDTH)
-                stacked = slice(j * SPAN, (j + 1) * SPAN)
-                q_s[g, half, stacked] = rotated(q_raw[rows, cols], half)
-                grad = g_raw[rows, cols]
-                g_s[g, half, stacked] = grad
-                product = grad.astype(F32) * o_raw[rows, cols].astype(F32)
-                upper = product.astype(BF16)
-                lower = (product - upper.astype(F32)).astype(BF16)
-                delta = dot(ones, upper, 1, 1) + dot(ones, lower, 1, 1)
-                delta_s[g, half, :, stacked] = delta
-                lse_s[g, half, :, stacked] = jnp.broadcast_to(
-                    lse_raw[head : head + 1, rows] * LOG2E, (8, SPAN)
-                )
+                q_s[g, half, j * SPAN : (j + 1) * SPAN] = rotated(q_raw[rows, cols], half)
+            if half == 1:
+                move(g, 0).start()
 
     step_cols = 2 * SPAN
 
-    def unit(g, q_half, key, value, causal=False, visible=None):
+    def unit(rows_of, key, value, causal=False, visible=None):
+        q_rows, g_rows, stat = rows_of
         value_sum = key_sum = None
         query_parts = []
         for start in range(0, share * SPAN, step_cols):
             at = slice(start, start + step_cols)
-            query = q_s[g, q_half, at]
-            grad = g_s[g, q_half, at]
-            norm = lse_s[g, q_half, 0:1, at]
+            query = q_rows[at]
+            grad = g_rows[at]
+            norm = stat[0:1, at]
             if visible is not None:
                 norm = jnp.where(visible, norm, 1e30)
             weights = jnp.exp2(dot(key, query, 1, 1) * (ROOT_SCALE * LOG2E) - norm)
@@ -293,7 +324,7 @@
                 query_at = lax.broadcasted_iota(jnp.int32, shape, 1) & (SPAN - 1)
                 weights = jnp.where(key_at <= query_at, weights, 0.0)
             weight_grad = dot(value, grad, 1, 1)
-            score_grad = weights * (weight_grad - delta_s[g, q_half, 0:1, at])
+            score_grad = weights * (weight_grad - stat[1:2, at])
             rounded_weights = weights.astype(BF16)
             rounded_grad = score_grad.astype(BF16)
             value_part = dot(rounded_weights, grad, 1, 0)
@@ -305,6 +336,9 @@
 
     my_span = span_ref[me]
 
+    def here(g, half):
+        return q_s.at[g, half], g_s.at[g, half], stat_s.at[g, half]
+
     begun = set()
 
     def add_query(g, half, value):
@@ -315,12 +349,12 @@
 
     def own_block(g):
         early, late = 2 * g, 2 * g + 1
-        dv, dk, dq = unit(g, 0, kv[0, early, 1], kv[0, early, 0], causal=True)
+        dv, dk, dq = unit(here(g, 0), kv[0, early, 1], kv[0, early, 0], causal=True)
         add_query(g, 0, dq)
-        dv_next, dk_next, dq = unit(g, 1, kv[0, early, 1], kv[0, early, 0])
+        dv_next, dk_next, dq = unit(here(g, 1), kv[0, early, 1], kv[0, early, 0])
         own[early, 0] = dv + dv_next
         own[early, 1] = dk + dk_next
-        dv, dk, dq_next = unit(g, 1, kv[0, late, 1], kv[0, late, 0], causal=True)
+        dv, dk, dq_next = unit(here(g, 1), kv[0, late, 1], kv[0, late, 0], causal=True)
         own[late, 0] = dv
         own[late, 1] = dk
         add_query(g, 1, dq + dq_next)
@@ -334,30 +368,41 @@
         lower = span_ref[lax.rem(me + hop, n_ctx)] < my_span
         key, value = kv[hop, chunk, 1], kv[hop, chunk, 0]
         if half == 0:
-            dv, dk, dq = unit(g, 1, key, value)
+            dv, dk, dq = unit(here(g, 1), key, value)
             add_query(g, 1, dq)
-            dv_next, dk_next, dq = unit(g, 0, key, value, visible=lower)
+            dv_next, dk_next, dq = unit(here(g, 0), key, value, visible=lower)
             add_query(g, 0, dq)
             sums = (dv + dv_next, dk + dk_next)
         else:
-            dv, dk, dq = unit(g, 1, key, value, visible=jnp.logical_not(lower))
+            dv, dk, dq = unit(here(g, 1), key, value, visible=jnp.logical_not(lower))
             add_query(g, 1, dq)
+            if hop == last_hop(chunk):
+                for what in range(3):
+                    move(g, what).wait_recv()
+                far_visible = span_ref[lax.rem(me + hop, n_ctx)] > span_ref[left]
+                dv_far, dk_far, dq_far = unit(
+                    (far_q.at[g], far_g.at[g], far_stat.at[g]), key, value, visible=far_visible
+                )
+                dv = dv + dv_far
+                dk = dk + dk_far
+                far_dq_send[g] = dq_far.astype(BF16)
             sums = (dv, dk)
         for which in range(2):
-            if hop == WIN - 1 or chunk in DIRECT:
+            if hop == last_hop(chunk):
                 ret_send[chunk, hop - 1, which] = sums[which].astype(BF16)
                 back(which, chunk, hop).start()
             else:
                 part[chunk, hop - 1, which] = sums[which]
+        if half == 1 and hop == last_hop(chunk):
+            move(g, 3).start()
 
     def back(which, chunk, hop):
-        target = lax.rem(me + hop, n_ctx) if chunk in DIRECT else right
         return pltpu.make_async_remote_copy(
             src_ref=ret_send.at[chunk, hop - 1, which],
             dst_ref=ret_recv.at[chunk, hop - 1, which],
             send_sem=ret_ssem.at[which, chunk, hop - 1],
             recv_sem=ret_rsem.at[which, chunk, hop - 1],
-            device_id=(target, my_head),
+            device_id=(right, my_head),
             device_id_type=MESH,
         )
 
@@ -377,6 +422,7 @@
         stores.append(copy)
 
     def finish_query(g):
+        move(g, 3).wait_recv()
         for half in range(2):
             rows = slice(half * SPAN, (half + 1) * SPAN)
             cosine = tab_t[0, :, rows] * ROOT_SCALE
@@ -385,6 +431,9 @@
                 stacked = slice(j * SPAN, (j + 1) * SPAN)
                 first = dq_acc[g, half, 0:HALF, stacked]
                 second = dq_acc[g, half, HALF:WIDTH, stacked]
+                if half == 1:
+                    first = first + far_dq_recv[g, 0:HALF, stacked].astype(F32)
+                    second = second + far_dq_recv[g, HALF:WIDTH, stacked].astype(F32)
                 turned = jnp.concatenate(
                     [first * cosine + second * sine, second * cosine - first * sine], axis=0
                 )
@@ -398,17 +447,14 @@
         rows = slice(half * SPAN, (half + 1) * SPAN)
         cols = slice(g * WIDTH, (g + 1) * WIDTH)
         for which, target in ((0, dv_hbm), (1, dk_hbm)):
-            total = own[chunk, which]
-            for hop in range(WIN - 1 if chunk in DIRECT else 1, 0, -1):
-                back(which, chunk, hop).wait_recv()
-                total = total + ret_recv[chunk, hop - 1, which].astype(F32)
+            back(which, chunk, 1).wait_recv()
+            total = own[chunk, which] + ret_recv[chunk, 0, which].astype(F32)
             if which == 1:
                 total = unrotated(total * ROOT_SCALE, half)
             dkv_out[which, rows, cols] = total.astype(BF16)
             store(dkv_out.at[which, rows, cols], target.at[rows, cols])
 
-    for name in ("q", "g", "o", "lse"):
-        loads[name].wait()
+    loads["q"].wait()
     for what, *at in ORDER:
         if what == "prepare":
             prepare(*at)
@@ -421,7 +467,7 @@
                 forward(which, chunk, hop + 1).start()
         elif what == "block":
             chunk, hop = at
-            if hop == WIN - 1:
+            if hop == last_hop(chunk):
                 got(chunk, hop)
             other_block(chunk, hop)
         elif what == "return":
@@ -435,9 +481,12 @@
         copy.wait_send()
     for chunk in range(chunks):
         for which in range(2):
-            for hop in range(1, WIN):
+            for hop in range(1, last_hop(chunk) + 1):
                 forward(which, chunk, hop).wait_send()
                 back(which, chunk, hop).wait_send()
+    for g in range(groups):
+        for what in range(4):
+            move(g, what).wait_send()
     for copy in stores:
         copy.wait()
 
@@ -472,10 +521,14 @@
             pltpu.VMEM((groups, 2, share * SPAN, WIDTH), BF16),
             pltpu.VMEM((groups, 2, share * SPAN, WIDTH), BF16),
             pltpu.VMEM((groups, 2, 8, share * SPAN), F32),
-            pltpu.VMEM((groups, 2, 8, share * SPAN), F32),
             pltpu.VMEM((2, HALF, rows), F32),
             pltpu.VMEM((2, rows, WIDTH), F32),
             pltpu.VMEM((WIN, chunks, 2, SPAN, WIDTH), BF16),
+            pltpu.VMEM((groups, share * SPAN, WIDTH), BF16),
+            pltpu.VMEM((groups, share * SPAN, WIDTH), BF16),
+            pltpu.VMEM((groups, 8, share * SPAN), F32),
+            pltpu.VMEM((groups, WIDTH, share * SPAN), BF16),
+            pltpu.VMEM((groups, WIDTH, share * SPAN), BF16),
             pltpu.VMEM((groups, 2, WIDTH, share * SPAN), F32),
             pltpu.VMEM((rows, heads * WIDTH), BF16),
             pltpu.VMEM((chunks, 2, SPAN, WIDTH), F32),
@@ -491,6 +544,8 @@
             dma((2, chunks, hops)),
             dma((2, chunks, hops)),
             dma((2, chunks, hops)),
+            dma((groups, 4)),
+            dma((groups, 4)),
         ],
         compiler_params=pltpu.CompilerParams(
             collective_id=0, has_side_effects=True, vmem_limit_bytes=40 * 2**20

time: 55.2 us -> 50.9 us (0.922)
  Pallas kernels: 52.3 us -> 47.8 us
    pallas_call x1, Pallas kernels: 52.3 us -> 47.8 us  [shards(): pl.pallas_call(functools.partial(kernel, groups, share, n_ctx, n_head), o...]
where the time goes in v3:
time: 50.9 us; the launch traced here: 50.6 us
  Pallas kernels  47.8 us (94%)
  local copies, waits for them, and re-layouts  2.11 us (4%)
  between operations  0.64 us (1%)
    pallas_call x1, Pallas kernels, shards(): pl.pallas_call(functools.partial(kernel, groups, share, n_ctx, n_head), o...  47.8 us
    unnamed x3, local copies, waits for them, and re-layouts  2.11 us

profile of v3, /device:TPU:2, one launch (start us, length us, event | category | flops | bytes accessed | tf_op | source)
XLA Modules:
  0.0 50.6 jit_solution(14807977508814305204)
XLA Ops:
  0.6 47.8 %shard_map.103 = (bf16[256,1024]{1,0:T(8,128)(2,1)S(1)}, bf16[256,256]{1,0:T(8,128)(2,1)S(1)}, bf16[256,256]{1,0:T(8,128)(2,1)S(1)}) custom-call(s32[64]{0:T(128)} %span_ref.1, bf16[256,1024]{1,0:T(8,128)(2,1)} %q_hbm.1, bf16[256,256]{1,0:T(8,128)(2,1)} %k_hbm.1, bf16[256,256]{1,0:T(8,128)(2,1)} %v_hbm.1, bf16[256,1024]{1,0:T(8,128)(2,1)} %g_hbm.1, ...), custom_call_target="tpu_custom_call" | custom-call | flops 1509949440 | bytes 2621440 | tf_op jit(solution)/shard_map/pallas_call | solution.py:505
  48.5 0.8 %copy.14 = bf16[256,1024]{1,0:T(8,128)(2,1)} copy(bf16[256,1024]{1,0:T(8,128)(2,1)S(1)} %get-tuple-element.6) | data formatting | bytes 1048576
  49.3 0.7 %copy.15 = bf16[256,256]{1,0:T(8,128)(2,1)} copy(bf16[256,256]{1,0:T(8,128)(2,1)S(1)} %get-tuple-element.7) | data formatting | bytes 262144
  49.9 0.7 %copy.16 = bf16[256,256]{1,0:T(8,128)(2,1)} copy(bf16[256,256]{1,0:T(8,128)(2,1)S(1)} %get-tuple-element.8) | data formatting | bytes 262144

commit v4 on v3

--- a/solution.py
+++ b/solution.py
@@ -24,38 +24,38 @@
 BF16 = jnp.bfloat16
 MESH = pl.DeviceIdType.MESH
 ORDER = (
+    ("prepare", 0),
     ("prepare", 1),
-    ("prepare", 0),
     ("own", 0),
     ("pass", 0, 1),
     ("pass", 2, 1),
     ("pass", 1, 1),
-    ("block", 2, 1),
+    ("own", 1),
     ("pass", 0, 2),
     ("block", 0, 2),
+    ("pass", 2, 2),
+    ("block", 2, 1),
     ("pass", 3, 1),
-    ("block", 3, 1),
-    ("block", 0, 1),
-    ("pass", 2, 2),
     ("block", 1, 2),
     ("block", 0, 3),
+    ("block", 2, 3),
     ("block", 3, 2),
-    ("block", 2, 3),
     ("block", 2, 2),
     ("return", 0, 2),
     ("block", 1, 1),
+    ("block", 3, 1),
+    ("return", 2, 2),
+    ("block", 0, 1),
+    ("return", 3, 1),
     ("return", 1, 1),
-    ("return", 2, 2),
+    ("return", 2, 1),
     ("return", 0, 1),
-    ("own", 1),
-    ("return", 3, 1),
+    ("query", 0),
+    ("query", 1),
+    ("keys", 2),
     ("keys", 1),
-    ("query", 1),
-    ("query", 0),
-    ("return", 2, 1),
+    ("keys", 3),
     ("keys", 0),
-    ("keys", 3),
-    ("keys", 2),
 )
 
 
@@ -118,9 +118,7 @@
     o_hbm,
     lse_hbm,
     pos_hbm,
-    dq_hbm,
-    dk_hbm,
-    dv_hbm,
+    out_ref,
     q_raw,
     k_raw,
     g_raw,
@@ -139,14 +137,11 @@
     far_dq_send,
     far_dq_recv,
     dq_acc,
-    dq_out,
     own,
     part,
     ret_send,
     ret_recv,
-    dkv_out,
     load_sem,
-    store_sem,
     pos_ssem,
     pos_rsem,
     fwd_ssem,
@@ -162,6 +157,11 @@
     right = lax.rem(me + 1, n_ctx)
     peers = [lax.rem(my_head + step, n_head) for step in range(1, n_head)]
 
+    barrier = pltpu.get_barrier_semaphore()
+    for ctx in (left, right):
+        pl.semaphore_signal(barrier, inc=1, device_id=(ctx, my_head), device_id_type=MESH)
+    for peer in peers:
+        pl.semaphore_signal(barrier, inc=1, device_id=(me, peer), device_id_type=MESH)
     loads = {}
 
     def load(name, index, source, target):
@@ -185,12 +185,53 @@
     load("o", base + 3, o_hbm, o_raw)
     load("lse", base + 4, lse_hbm, lse_raw)
 
-    barrier = pltpu.get_barrier_semaphore()
-    for ctx in (left, right):
-        pl.semaphore_signal(barrier, inc=1, device_id=(ctx, my_head), device_id_type=MESH)
-    for peer in peers:
-        pl.semaphore_signal(barrier, inc=1, device_id=(me, peer), device_id_type=MESH)
     freq = frequencies((HALF, WIDTH))
+    loads["pos"].wait()
+    pl.semaphore_wait(barrier, 2 + len(peers))
+
+    pos_copies = []
+    for step, peer in enumerate(peers):
+        copy = pltpu.make_async_remote_copy(
+            src_ref=pos_all.at[my_head],
+            dst_ref=pos_all.at[my_head],
+            send_sem=pos_ssem.at[step],
+            recv_sem=pos_rsem.at[step],
+            device_id=(me, peer),
+            device_id_type=MESH,
+        )
+        copy.start()
+        pos_copies.append(copy)
+
+    def forward(which, chunk, hop):
+        return pltpu.make_async_remote_copy(
+            src_ref=kv.at[hop - 1, chunk, which],
+            dst_ref=kv.at[hop, chunk, which],
+            send_sem=fwd_ssem.at[which, chunk, hop - 1],
+            recv_sem=fwd_rsem.at[which, chunk, hop - 1],
+            device_id=(left, my_head),
+            device_id_type=MESH,
+        )
+
+    def move(g, what):
+        source, target, place = (
+            (q_s.at[g, 1], far_q.at[g], right),
+            (g_s.at[g, 1], far_g.at[g], right),
+            (stat_s.at[g, 1], far_stat.at[g], right),
+            (far_dq_send.at[g], far_dq_recv.at[g], left),
+        )[what]
+        return pltpu.make_async_remote_copy(
+            src_ref=source,
+            dst_ref=target,
+            send_sem=far_ssem.at[g, what],
+            recv_sem=far_rsem.at[g, what],
+            device_id=(place, my_head),
+            device_id_type=MESH,
+        )
+
+    for chunk in range(chunks):
+        loads[("v", chunk)].wait()
+        forward(0, chunk, 1).start()
+
     for name in ("g", "o", "lse"):
         loads[name].wait()
     for g in range(groups):
@@ -210,52 +251,6 @@
                 norm = lse_raw[head : head + 1, rows] * LOG2E
                 first = lax.broadcasted_iota(jnp.int32, (8, SPAN), 0) == 0
                 stat_s[g, half, :, stacked] = jnp.where(first, norm, delta)
-    loads["pos"].wait()
-    pl.semaphore_wait(barrier, 2 + len(peers))
-
-    pos_copies = []
-    for step, peer in enumerate(peers):
-        copy = pltpu.make_async_remote_copy(
-            src_ref=pos_all.at[my_head],
-            dst_ref=pos_all.at[my_head],
-            send_sem=pos_ssem.at[step],
-            recv_sem=pos_rsem.at[step],
-            device_id=(me, peer),
-            device_id_type=MESH,
-        )
-        copy.start()
-        pos_copies.append(copy)
-
-    def forward(which, chunk, hop):
-        return pltpu.make_async_remote_copy(
-            src_ref=kv.at[hop - 1, chunk, which],
-            dst_ref=kv.at[hop, chunk, which],
-            send_sem=fwd_ssem.at[which, chunk, hop - 1],
-            recv_sem=fwd_rsem.at[which, chunk, hop - 1],
-            device_id=(left, my_head),
-            device_id_type=MESH,
-        )
-
-    def move(g, what):
-        source, target, place = (
-            (q_s.at[g, 1], far_q.at[g], right),
-            (g_s.at[g, 1], far_g.at[g], right),
-            (stat_s.at[g, 1], far_stat.at[g], right),
-            (far_dq_send.at[g], far_dq_recv.at[g], left),
-        )[what]
-        return pltpu.make_async_remote_copy(
-            src_ref=source,
-            dst_ref=target,
-            send_sem=far_ssem.at[g, what],
-            recv_sem=far_rsem.at[g, what],
-            device_id=(place, my_head),
-            device_id_type=MESH,
-        )
-
-    for chunk in range(chunks):
-        loads[("v", chunk)].wait()
-        forward(0, chunk, 1).start()
-    for g in range(groups):
         move(g, 1).start()
         move(g, 2).start()
 
@@ -414,13 +409,6 @@
             ).astype(BF16)
             back(which, chunk, hop).start()
 
-    stores = []
-
-    def store(source, target):
-        copy = pltpu.make_async_copy(source, target, store_sem.at[len(stores)])
-        copy.start()
-        stores.append(copy)
-
     def finish_query(g):
         move(g, 3).wait_recv()
         for half in range(2):
@@ -438,21 +426,18 @@
                     [first * cosine + second * sine, second * cosine - first * sine], axis=0
                 )
                 head = g * share + j
-                dq_out[rows, head * WIDTH : (head + 1) * WIDTH] = turned.T.astype(BF16)
-        cols = slice(g * share * WIDTH, (g + 1) * share * WIDTH)
-        store(dq_out.at[:, cols], dq_hbm.at[:, cols])
+                out_ref[rows, head * WIDTH : (head + 1) * WIDTH] = turned.T.astype(BF16)
 
     def finish_keys(chunk):
         g, half = chunk // 2, chunk % 2
         rows = slice(half * SPAN, (half + 1) * SPAN)
-        cols = slice(g * WIDTH, (g + 1) * WIDTH)
-        for which, target in ((0, dv_hbm), (1, dk_hbm)):
+        for which in range(2):
             back(which, chunk, 1).wait_recv()
             total = own[chunk, which] + ret_recv[chunk, 0, which].astype(F32)
             if which == 1:
                 total = unrotated(total * ROOT_SCALE, half)
-            dkv_out[which, rows, cols] = total.astype(BF16)
-            store(dkv_out.at[which, rows, cols], target.at[rows, cols])
+            place = (groups * share + groups * (1 - which) + g) * WIDTH
+            out_ref[rows, place : place + WIDTH] = total.astype(BF16)
 
     loads["q"].wait()
     for what, *at in ORDER:
@@ -487,8 +472,6 @@
     for g in range(groups):
         for what in range(4):
             move(g, what).wait_send()
-    for copy in stores:
-        copy.wait()
 
 
 def shards(query, key, value, out_grad, attn_out, log_sum_exp, positions, span_map):
@@ -502,15 +485,11 @@
     chunks = 2 * groups
     dma = pltpu.SemaphoreType.DMA
     anywhere = pl.BlockSpec(memory_space=pl.ANY)
-    return pl.pallas_call(
+    merged = pl.pallas_call(
         functools.partial(kernel, groups, share, n_ctx, n_head),
-        out_shape=(
-            jax.ShapeDtypeStruct((rows, heads * WIDTH), BF16),
-            jax.ShapeDtypeStruct((rows, groups * WIDTH), BF16),
-            jax.ShapeDtypeStruct((rows, groups * WIDTH), BF16),
-        ),
+        out_shape=jax.ShapeDtypeStruct((rows, (heads + 2 * groups) * WIDTH), BF16),
         in_specs=[pl.BlockSpec(memory_space=pltpu.SMEM)] + [anywhere] * 7,
-        out_specs=(anywhere,) * 3,
+        out_specs=pl.BlockSpec(memory_space=pltpu.VMEM),
         scratch_shapes=[
             pltpu.VMEM((rows, heads * WIDTH), BF16),
             pltpu.VMEM((rows, groups * WIDTH), BF16),
@@ -530,14 +509,11 @@
             pltpu.VMEM((groups, WIDTH, share * SPAN), BF16),
             pltpu.VMEM((groups, WIDTH, share * SPAN), BF16),
             pltpu.VMEM((groups, 2, WIDTH, share * SPAN), F32),
-            pltpu.VMEM((rows, heads * WIDTH), BF16),
             pltpu.VMEM((chunks, 2, SPAN, WIDTH), F32),
             pltpu.VMEM((chunks, hops - 1, 2, SPAN, WIDTH), F32),
             pltpu.VMEM((chunks, hops, 2, SPAN, WIDTH), BF16),
             pltpu.VMEM((chunks, hops, 2, SPAN, WIDTH), BF16),
-            pltpu.VMEM((2, rows, groups * WIDTH), BF16),
             dma((6 + chunks,)),
-            dma((groups + 2 * chunks,)),
             dma((n_head - 1,)),
             dma((n_head - 1,)),
             dma((2, chunks, hops)),
@@ -563,6 +539,8 @@
             )
         ),
     )
+    first, second = heads * WIDTH, (heads + groups) * WIDTH
+    return merged[:, :first], merged[:, first:second], merged[:, second:]
 
 
 def solution(mesh):

time: 50.9 us -> 50.2 us (0.986)
  local copies, waits for them, and re-layouts: 2.11 us -> 1.58 us
    unnamed x3 -> x0, local copies, waits for them, and re-layouts: 2.11 us -> none
    slice x0 -> x2, local copies, waits for them, and re-layouts: none -> 1.58 us  [shards(): return (merged[:, :first], merged[:, first:second], merged[:, second:])]
where the time goes in v4:
time: 50.2 us; the launch traced here: 49.8 us
  Pallas kernels  47.6 us (95%)
  local copies, waits for them, and re-layouts  1.58 us (3%)
  between operations  0.64 us (1%)
    pallas_call x1, Pallas kernels, shards(): pl.pallas_call(functools.partial(kernel, groups, share, n_ctx, n_head), o...  47.6 us
    slice x2, local copies, waits for them, and re-layouts, shards(): return (merged[:, :first], merged[:, first:second], merged[:, second:])  1.58 us

profile of v4, /device:TPU:2, one launch (start us, length us, event | category | flops | bytes accessed | tf_op | source)
XLA Modules:
  0.0 49.8 jit_solution(841814690356781501)
XLA Ops:
  0.6 47.6 %shard_map.103 = bf16[256,1536]{1,0:T(8,128)(2,1)S(1)} custom-call(s32[64]{0:T(128)} %span_ref.1, bf16[256,1024]{1,0:T(8,128)(2,1)} %q_hbm.1, bf16[256,256]{1,0:T(8,128)(2,1)} %k_hbm.1, bf16[256,256]{1,0:T(8,128)(2,1)} %v_hbm.1, bf16[256,1024]{1,0:T(8,128)(2,1)} %g_hbm.1, bf16[256,1024]{1,0:T(8,128)(2,1)} %o_hbm.1, f32[8,256]{1,0:T(8,128)} %lse_hbm.1, ...), custom_call_target="tpu_custom_call" | custom-call | flops 1509949440 | bytes 2621440 | tf_op jit(solution)/shard_map/pallas_call | solution.py:488
  48.2 0.7 %fusion = (bf16[256,256]{1,0:T(8,128)(2,1)}, bf16[256,256]{1,0:T(8,128)(2,1)}) fusion(bf16[256,1536]{1,0:T(8,128)(2,1)S(1)} %shard_map.103), kind=kLoop, calls=%fused_computation | loop fusion | bytes 524288 | tf_op jit(solution)/shard_map/slice | solution.py:543
  48.9 0.9 %slice.9 = bf16[256,1024]{1,0:T(8,128)(2,1)} slice(bf16[256,1536]{1,0:T(8,128)(2,1)S(1)} %shard_map.103), slice={[0:256], [0:1024]} | slice | bytes 1048576 | tf_op jit(solution)/shard_map/slice | solution.py:543
